TPU v7x, 512 devices: a whole 4x4x16 slice. The times are simulated.
512 devices in a mesh: wide: 128 (over z, y, core), tm: 4 (over x).
Axes of the slice: x: 4, y: 4, z: 16, core: 2. Of those that a mesh axis runs over, the one named last changes fastest.
Arguments:
- voltages: bfloat16 [2, 1024, 131072], P(None, 'wide', 'tm'), may hold values from -6 to 6
- filter_taps: float32 [12, 256], replicated, may hold values from -1.75 to 1.75
- stations: int32 [4, 128], replicated, may hold values from 0 to 511, as said below
- allocation: int32 [4, 256], replicated, may hold values 0 or 1
Outputs:
- visibilities: float32 [4, 256, 2, 256, 256], P('tm', 'wide')
Inputs may be any that keep to these rules, and one draw needn't show every extreme that they name: `stations`: every station belongs to exactly one subarray.
All inputs are finite; a program needn't handle non-finite values.
Results may differ from a plain program's by a relative error of at most 0.0039.
Values may be sent and summed in bfloat16 or wider, within the bound.
No kernel may reach another device: no remote copies, remote signals or barrier semaphores. Data moves between devices by JAX's collectives and lax.ppermute only.
A program may use at most 64 MiB of HBM per device.

v0:
```python
import math

import jax
import jax.numpy as jnp
from jax import lax
from jax.sharding import PartitionSpec as P


def shifted(value, axis, steps):
    count = lax.axis_size(axis)
    initial, last = (max(0, -steps), min(count, count - steps))
    return lax.ppermute(value, axis, [(source, source + steps) for source in range(initial, last)])


def make_tables(length):
    grid = (
        jnp.arange(length, dtype=jnp.int32)[:, None]
        * jnp.arange(length, dtype=jnp.int32)[None, :]
        % length
    )
    angle = grid.astype(jnp.float32) * (2.0 * math.pi / length)
    scale = 1.0 / math.sqrt(length)
    return (
        (jnp.cos(angle) * scale).astype(jnp.bfloat16),
        (jnp.sin(angle) * scale).astype(jnp.bfloat16),
    )


def correlate(chosen, scale):
    real_sel = chosen[0]
    imaginary_picked = chosen[1]
    gram_real = jnp.einsum(
        "csif,csjf->scij", real_sel, real_sel, preferred_element_type=jnp.float32
    ) + jnp.einsum(
        "csif,csjf->scij", imaginary_picked, imaginary_picked, preferred_element_type=jnp.float32
    )
    gram_imag = jnp.einsum(
        "csif,csjf->scij", imaginary_picked, real_sel, preferred_element_type=jnp.float32
    ) - jnp.einsum(
        "csif,csjf->scij", real_sel, imaginary_picked, preferred_element_type=jnp.float32
    )
    return jnp.stack([gram_real, gram_imag], axis=2) * scale


def shards(voltages, filter_taps, stations, allocation):
    num_taps, length = filter_taps.shape
    signals = voltages.shape[1]
    frames = voltages.shape[2] // length
    segments = lax.axis_size("tm")
    signal = voltages.reshape(2, signals, frames, length)
    earlier = shifted(signal[:, :, frames - (num_taps - 1) :, :], "tm", 1)
    padded = jnp.concatenate([earlier, signal], axis=2)
    summed = jnp.zeros((2, signals, frames, length), jnp.float32)
    for tap in range(num_taps):
        summed = summed + filter_taps[tap] * padded[:, :, tap : tap + frames, :].astype(jnp.float32)
    filter_output = summed.astype(jnp.bfloat16)
    cosine_lookup, sin_table = make_tables(length)
    real_component = jnp.einsum(
        "ck,sfk->csf", cosine_lookup, filter_output[0], preferred_element_type=jnp.float32
    ) + jnp.einsum("ck,sfk->csf", sin_table, filter_output[1], preferred_element_type=jnp.float32)
    imaginary_component = jnp.einsum(
        "ck,sfk->csf", cosine_lookup, filter_output[1], preferred_element_type=jnp.float32
    ) - jnp.einsum("ck,sfk->csf", sin_table, filter_output[0], preferred_element_type=jnp.float32)
    spectra = jnp.stack([real_component, imaginary_component]).astype(jnp.bfloat16)
    turned = lax.all_to_all(spectra, "wide", split_axis=1, concat_axis=2, tiled=True)
    ch_dev = turned.shape[1]
    first_chan = lax.axis_index("wide") * ch_dev
    num_subs, sub_size = stations.shape
    rows = (2 * stations[:, :, None] + jnp.arange(2, dtype=jnp.int32)[None, None, :]).reshape(
        num_subs, 2 * sub_size
    )
    chosen = jnp.take(turned, rows, axis=2)
    window_weights = lax.dynamic_slice_in_dim(allocation, first_chan, ch_dev, 1).astype(jnp.float32)
    scale = 1.0 / (frames * segments)
    grams = correlate(chosen, scale) * window_weights[:, :, None, None, None]
    return lax.psum_scatter(grams, "tm", scatter_dimension=0, tiled=True)


def solution(mesh):
    return jax.shard_map(
        shards,
        mesh=mesh,
        in_specs=(P(None, "wide", "tm"), P(), P(), P()),
        out_specs=P("tm", "wide", None, None, None),
        check_vma=False,
    )
```

profile of v0, /device:TPU:24, one launch (start us, length us, event | category | flops | bytes accessed | tf_op | source)
XLA Modules:
  0.0 220.8 jit_solution(5667313318528633616)
XLA Ops:
  6.5 0.0 copy-start
  6.5 1.5 copy.61
  8.0 3.4 %collective-permute-start = (bf16[2,8,11,256]{3,2,1,0:T(8,128)(2,1)S(1)}, bf16[2,8,11,256]{3,2,1,0:T(8,128)(2,1)S(1)}, u32[]{:S(2)}, u32[]{:S(2)}) collective-permute-start(bf16[2,8,11,256]{3,2,1,0:T(8,128)(2,1)S(1)} %slice.116), channel_id=1, source_target_pairs={{0,1},{1,2},{2,3},{4,5},{5,6},{6,7},{8,9},{9,10},{10,11},{12,13},{... | collective-permute-start | bytes 270344 | tf_op jit(solution)/shard_map/ppermute | solution.py:12
  11.5 0.0 copy-done
  11.5 2.7 %collective-permute-done = bf16[2,8,11,256]{3,2,1,0:T(8,128)(2,1)S(1)} collective-permute-done((bf16[2,8,11,256]{3,2,1,0:T(8,128)(2,1)S(1)}, bf16[2,8,11,256]{3,2,1,0:T(8,128)(2,1)S(1)}, u32[]{:S(2)}, u32[]{:S(2)}) %collective-permute-start) | collective-permute-done | bytes 90144 | tf_op jit(solution)/shard_map/ppermute | solution.py:12
  14.2 3.5 %add_convert_fusion = bf16[2,8,128,256]{3,2,1,0:T(8,128)(2,1)S(1)} fusion(bf16[2,8,128,256]{3,2,1,0:T(8,128)(2,1)S(1)} %copy.61, bf16[2,8,11,256]{3,2,1,0:T(8,128)(2,1)S(1)} %collective-permute-done, f32[256]{0:T(256)S(1)} %bitcast.93, f32[256]{0:T(256)S(1)} %bitcast.94, f32[256]{0:T(256)S(1)} %bitcast.84, f32[256]{0:T(256)S(1)} %bitcast.85, ...), kind=kLoop, calls=%fused_computation.14 | loop fusion | flops 36175872 | bytes 2199552 | tf_op jit(solution)/shard_map/convert_element_type | solution.py:56
  17.7 1.2 fusion.15
  18.9 1.2 fusion.16
  20.2 1.2 fusion.3
  21.4 1.2 fusion.2
  22.6 0.1 pad_maximum_fusion.1
  22.7 0.0 copy-start.1
  22.8 0.0 copy-start.2
  22.8 1.6 copy.41
  24.4 19.3 %all-to-all-start = ((bf16[2,256,8,128]{3,2,0,1:T(8,128)(2,1)}), bf16[2,256,8,128]{3,2,0,1:T(8,128)(2,1)S(1)}, u32[]{:S(2)}, u32[]{:S(2)}) async-start(bf16[2,256,8,128]{3,2,0,1:T(8,128)(2,1)} %copy.41), calls=%async_computation | async-start | bytes 2097152 | tf_op jit(solution)/shard_map/all_to_all | solution.py:65
  43.7 0.2 all-reduce.3.cloned.1.call-start
  43.9 0.0 copy-done.1
  44.0 0.1 copy.39
  44.1 0.1 add.119
  44.3 0.1 compare_select_fusion
  44.4 0.1 copy.44
  44.5 0.1 copy.40
  44.6 0.0 copy-done.2
  44.6 0.1 convert_multiply_fusion
  44.7 53.6 %all-to-all-done = bf16[2,256,8,128]{3,2,0,1:T(8,128)(2,1)S(1)} async-done(((bf16[2,256,8,128]{3,2,0,1:T(8,128)(2,1)}), bf16[2,256,8,128]{3,2,0,1:T(8,128)(2,1)S(1)}, u32[]{:S(2)}, u32[]{:S(2)}) %all-to-all-start) | async-done | bytes 1048608 | tf_op jit(solution)/shard_map/all_to_all | solution.py:65
  98.3 0.2 copy.62
  98.5 1.1 copy.45
  99.5 5.0 %gather_fusion = bf16[1024,2,2,128]{3,2,1,0:T(2,128)(2,1)S(1)} fusion(bf16[2,2,1024,128]{3,1,2,0:T(2,128)(2,1)S(1)} %copy.45, s32[1024]{0:T(1024)S(1)} %broadcast_clamp_fusion), kind=kCustom, calls=%fused_computation | custom fusion | bytes 2101248 | tf_op jit(solution)/shard_map/jit(_take)/gather | solution.py:72
  104.6 0.2 fusion.14
  104.8 0.4 fusion.18
  105.2 0.4 fusion.17
  105.7 0.4 add_bitcast_fusion
  106.1 0.4 subtract_bitcast_fusion
  106.6 2.6 %maximum_multiply_fusion = f32[4,2,2,256,256]{4,3,1,0,2:T(8,128)} fusion(f32[4,2,1,256,256]{4,3,1,0,2:T(8,128)S(1)} %subtract_bitcast_fusion, f32[4,2,1,256,256]{4,3,1,0,2:T(8,128)S(1)} %add_bitcast_fusion, f32[4,2]{1,0:T(4,128)S(1)} %convert_multiply_fusion), kind=kLoop, calls=%fused_computation.11 | loop fusion | flops 2097152 | bytes 8388640 | tf_op jit(solution)/shard_map/mul | solution.py:75
  109.1 0.0 all-reduce.3.cloned.1.call-update
  109.2 1.3 dynamic-slice
  110.4 100.5 %all-reduce.3.cloned.1.call-done = f32[4,2,2,256,256]{4,3,1,0,2:T(8,128)} async-done(((f32[4,2,2,256,256]{4,3,1,0,2:T(8,128)}), f32[4,2,2,256,256]{4,3,1,0,2:T(8,128)}) %all-reduce.3.cloned.1.call-update) | async-done | bytes 4194320
  210.9 2.0 constant_dynamic-slice_fusion
  212.9 1.0 copy.48
  (8 shorter events, 0.1 us)
Async XLA Ops:
  6.5 4.9 %copy-start = (f32[12,256]{1,0:T(8,128)S(1)}, f32[12,256]{1,0:T(8,128)}, u32[]{:S(2)}) copy-start(f32[12,256]{1,0:T(8,128)} %param.5) | copy-start | bytes 36868
  8.0 6.1 %collective-permute-start = (bf16[2,8,11,256]{3,2,1,0:T(8,128)(2,1)S(1)}, bf16[2,8,11,256]{3,2,1,0:T(8,128)(2,1)S(1)}, u32[]{:S(2)}, u32[]{:S(2)}) collective-permute-start(bf16[2,8,11,256]{3,2,1,0:T(8,128)(2,1)S(1)} %slice.116), channel_id=1, source_target_pairs={{0,1},{1,2},{2,3},{4,5},{5,6},{6,7},{8,9},{9,10},{10,11},{12,13},{... | collective-permute-start | bytes 270344 | tf_op jit(solution)/shard_map/ppermute | solution.py:12
  22.7 21.2 %copy-start.1 = (s32[4,128]{1,0:T(4,128)S(1)}, s32[4,128]{1,0:T(4,128)}, u32[]{:S(2)}) copy-start(s32[4,128]{1,0:T(4,128)} %param.6) | copy-start | bytes 6148
  22.8 21.8 %copy-start.2 = (s32[4,256]{1,0:T(4,128)S(1)}, s32[4,256]{1,0:T(4,128)}, u32[]{:S(2)}) copy-start(s32[4,256]{1,0:T(4,128)} %param.7) | copy-start | bytes 12292
  24.4 73.9 %all-to-all-start = ((bf16[2,256,8,128]{3,2,0,1:T(8,128)(2,1)}), bf16[2,256,8,128]{3,2,0,1:T(8,128)(2,1)S(1)}, u32[]{:S(2)}, u32[]{:S(2)}) async-start(bf16[2,256,8,128]{3,2,0,1:T(8,128)(2,1)} %copy.41), calls=%async_computation | async-start | bytes 2097152 | tf_op jit(solution)/shard_map/all_to_all | solution.py:65
  43.7 167.2 %all-reduce.3.cloned.1.call-start = ((), (), s32[]{:S(2)}) async-start(), calls=%async_computation.1 | async-start | bytes 8388608
Sparse Core Ops, SparseCore 0:
  109.3 101.5 all-reduce.2
where the time goes:
time: 222 us; the launch traced here: 221 us
  waiting for transfers between devices  157 us (71%)
  starting transfers between devices  22.9 us (10%)
  local copies, waits for them, and re-layouts  14.2 us (6%)
  between operations  13.6 us (6%)
  other arithmetic  6.61 us (3%)
  matrix products  6.61 us (3%)
    unnamed x2, waiting for transfers between devices  100 us
    all_to_all x1, waiting for transfers between devices, shards(): lax.all_to_all(spectra, 'wide', split_axis=1, concat_axis=2, tiled=True)  53.6 us
    all_to_all x1, starting transfers between devices, shards(): lax.all_to_all(spectra, 'wide', split_axis=1, concat_axis=2, tiled=True)  19.3 us
    gather x1, local copies, waits for them, and re-layouts, shards(): chosen = jnp.take(turned, rows, axis=2)  5.04 us
    unnamed x10, local copies, waits for them, and re-layouts  4.71 us
  transfers between devices with their start and end apart: 3, of which 3 were waited for; matrix products, arithmetic and copies ran while one was open for 1% of the time, Pallas kernels for 0%

commit v1 on v0

v1 whole, which is shorter than its diff:
```python
import math

import jax
import jax.numpy as jnp
import numpy as np
from jax import lax
from jax.experimental import pallas as pl
from jax.experimental.pallas import tpu as pltpu
from jax.sharding import PartitionSpec as P

LANES = 128
SUBLANES = 8
BLOCK = 16


def shifted(value, axis, steps):
    count = lax.axis_size(axis)
    initial, last = (max(0, -steps), min(count, count - steps))
    return lax.ppermute(value, axis, [(source, source + steps) for source in range(initial, last)])


def transform_table(length):
    grid = np.arange(length)[:, None] * np.arange(length)[None, :] % length
    angle = grid * (2.0 * math.pi / length)
    scale = 1.0 / math.sqrt(length)
    cosine, sine = np.cos(angle) * scale, np.sin(angle) * scale
    real = np.concatenate([cosine, sine], axis=1)
    imaginary = np.concatenate([-sine, cosine], axis=1)
    table = np.stack([real, imaginary], axis=1).reshape(2 * length, 2 * length)
    return table.astype(jnp.bfloat16)


def channelize_kernel(x_ref, halo_ref, taps_ref, table_ref, out_ref, filtered, turned):
    taps, length = taps_ref.shape
    signals = x_ref.shape[1]
    frames = x_ref.shape[2] // length
    cols = length // LANES

    def load(ref, part, frame, col):
        start = pl.multiple_of((frame * cols + col) * LANES, LANES)
        return ref[part, :, pl.ds(start, LANES)].astype(jnp.float32)

    for part in range(2):
        for col in range(cols):
            weights = [
                jnp.broadcast_to(taps_ref[tap : tap + 1, col * LANES : (col + 1) * LANES], (signals, LANES))
                for tap in range(taps)
            ]

            def filter_block(window, first, part=part, col=col, weights=weights):
                for frame in range(BLOCK):
                    total = weights[0] * window[frame]
                    for tap in range(1, taps):
                        total = total + weights[tap] * window[frame + tap]
                    filtered[part, col, pl.ds(first + frame, signals, stride=frames), :] = total

            opening = [load(halo_ref, part, frame, col) for frame in range(taps - 1)]
            opening += [load(x_ref, part, frame, col) for frame in range(BLOCK)]
            filter_block(opening, 0)

            def step(block, carry, part=part, col=col, filter_block=filter_block):
                first = block * BLOCK
                window = [
                    load(x_ref, part, first - (taps - 1) + frame, col) for frame in range(BLOCK + taps - 1)
                ]
                filter_block(window, first)
                return carry

            lax.fori_loop(1, frames // BLOCK, step, 0)

    rows = table_ref.shape[0]
    for pair in range(signals // 2):
        span = slice(pair * 2 * frames, (pair + 1) * 2 * frames)
        samples = jnp.concatenate(
            [filtered[part, col, span, :] for part in range(2) for col in range(cols)], axis=1
        ).astype(jnp.bfloat16)
        spectrum = lax.dot_general(
            table_ref[...], samples, (((1,), (1,)), ((), ())), preferred_element_type=jnp.float32
        )
        for which in range(2):
            turned[pl.ds(pair * 2 + which, rows, stride=signals), :] = spectrum[
                :, which * frames : (which + 1) * frames
            ]
    out_ref[...] = turned[...].astype(jnp.bfloat16).reshape(out_ref.shape)


def channelize(signal, halo, filter_taps, table):
    _, signals, samples = signal.shape
    length = filter_taps.shape[1]
    frames = samples // length
    rows = table.shape[0]
    return pl.pallas_call(
        channelize_kernel,
        out_shape=jax.ShapeDtypeStruct((rows, signals, frames), jnp.bfloat16),
        scratch_shapes=[
            pltpu.VMEM((2, length // LANES, signals * frames, LANES), jnp.float32),
            pltpu.VMEM((rows * signals, frames), jnp.float32),
        ],
        compiler_params=pltpu.CompilerParams(vmem_limit_bytes=24 * 1024 * 1024),
        cost_estimate=pl.CostEstimate(flops=600_000_000, bytes_accessed=3_000_000, transcendentals=0),
        name="channelize",
    )(signal, halo, filter_taps, table)


def choose_kernel(pick_ref, x_ref, out_ref):
    sources, parts, signals, frames = x_ref.shape
    columns = jnp.concatenate(
        [x_ref[:, part].reshape(sources * signals, frames) for part in range(parts)], axis=1
    )
    subs, _, members, _ = out_ref.shape
    for sub in range(subs):
        chosen = jnp.dot(
            pick_ref[sub * members : (sub + 1) * members, :], columns, preferred_element_type=jnp.float32
        ).astype(jnp.bfloat16)
        for part in range(parts):
            out_ref[sub, part] = chosen[:, part * frames : (part + 1) * frames]


def choose(pick, turned, subs):
    sources, parts, signals, frames = turned.shape
    members = sources * signals // subs
    return pl.pallas_call(
        choose_kernel,
        out_shape=jax.ShapeDtypeStruct((subs, parts, members, frames), jnp.bfloat16),
        compiler_params=pltpu.CompilerParams(vmem_limit_bytes=24 * 1024 * 1024),
        cost_estimate=pl.CostEstimate(flops=1_100_000_000, bytes_accessed=4_000_000, transcendentals=0),
        name="choose",
    )(pick, turned)


def correlate_kernel(weight_ref, x_ref, out_ref):
    segments, parts, _, _ = x_ref.shape
    for channel in range(parts // 2):
        real = [x_ref[segment, 2 * channel] for segment in range(segments)]
        imag = [x_ref[segment, 2 * channel + 1] for segment in range(segments)]
        left = jnp.concatenate(real + imag, axis=1)
        turned = jnp.concatenate(imag + [-value for value in real], axis=1)
        contract = (((1,), (1,)), ((), ()))
        weight = weight_ref[channel]
        out_ref[0, channel, 0] = weight * lax.dot_general(left, left, contract, preferred_element_type=jnp.float32)
        out_ref[0, channel, 1] = weight * lax.dot_general(turned, left, contract, preferred_element_type=jnp.float32)


def correlate(weights, gathered):
    segments, parts, members, frames = gathered.shape
    return pl.pallas_call(
        correlate_kernel,
        out_shape=jax.ShapeDtypeStruct((1, parts // 2, 2, members, members), jnp.float32),
        in_specs=[pl.BlockSpec(memory_space=pltpu.SMEM), pl.BlockSpec(memory_space=pltpu.VMEM)],
        compiler_params=pltpu.CompilerParams(vmem_limit_bytes=24 * 1024 * 1024),
        cost_estimate=pl.CostEstimate(flops=600_000_000, bytes_accessed=2_000_000, transcendentals=0),
        name="correlate",
    )(weights, gathered)


def shards(voltages, filter_taps, stations, allocation):
    num_taps, length = filter_taps.shape
    signals = voltages.shape[1]
    frames = voltages.shape[2] // length
    segments = lax.axis_size("tm")
    owners = lax.axis_size("wide")
    num_subs, sub_size = stations.shape
    halo = shifted(voltages[:, :, (frames - (num_taps - 1)) * length :], "tm", 1)
    table = jnp.asarray(transform_table(length))
    spectra = channelize(voltages, halo, filter_taps, table)
    ch_dev = length // owners
    spectra = spectra.reshape(owners, 2 * ch_dev, signals, frames)
    turned = lax.all_to_all(spectra, "wide", split_axis=0, concat_axis=0, tiled=True)
    rows = (2 * stations[:, :, None] + jnp.arange(2, dtype=jnp.int32)[None, None, :]).reshape(-1, 1)
    pick = (rows == jnp.arange(owners * signals, dtype=jnp.int32)[None, :]).astype(jnp.bfloat16)
    chosen = choose(pick, turned, num_subs)
    gathered = lax.all_to_all(chosen, "tm", split_axis=0, concat_axis=0, tiled=True)
    first_chan = lax.axis_index("wide") * ch_dev
    sub = lax.axis_index("tm")
    mine = lax.dynamic_slice(allocation, (sub, first_chan), (1, ch_dev)).reshape(ch_dev)
    weights = mine.astype(jnp.float32) * (1.0 / (frames * segments))
    return correlate(weights, gathered)


def solution(mesh):
    return jax.shard_map(
        shards,
        mesh=mesh,
        in_specs=(P(None, "wide", "tm"), P(), P(), P()),
        out_specs=P("tm", "wide", None, None, None),
        check_vma=False,
    )
```

time: 222 us -> 114 us (0.51)
  waiting for transfers between devices: 157 us -> 70.5 us
  between operations: 13.6 us -> 0.06 us
  local copies, waits for them, and re-layouts: 14.2 us -> 4.06 us
  Pallas kernels: 0 us -> 8.62 us
  matrix products: 6.61 us -> 0 us
  other arithmetic: 6.61 us -> 1.3 us
  starting transfers between devices: 22.9 us -> 27.9 us
    unnamed x2 -> x0, waiting for transfers between devices: 100 us -> none
    all_to_all x1 -> x2, waiting for transfers between devices: 53.6 us -> 68.4 us  [the longest x1 53.8 us: shards(): lax.all_to_all(spectra, 'wide', split_axis=0, concat_axis=0, tiled=True)]
    pallas_call x0 -> x3, Pallas kernels: none -> 8.62 us  [the longest x1 4.15 us: channelize(): pl.pallas_call(channelize_kernel, out_shape=jax.ShapeDtypeStruct((rows, s...]
    dot_general x8 -> x0, matrix products: 6.61 us -> none  [the longest x1 1.23 us: shards(): jnp.einsum('ck,sfk->csf', sin_table, filter_output[1], preferred_element_...]
    all_to_all x1 -> x2, starting transfers between devices: 19.3 us -> 24.5 us  [the longest x1 19.3 us: shards(): lax.all_to_all(spectra, 'wide', split_axis=0, concat_axis=0, tiled=True)]
    gather x1 -> x0, local copies, waits for them, and re-layouts: 5.04 us -> none  [shards(): chosen = jnp.take(turned, rows, axis=2)]
    convert_element_type x1, other arithmetic: 3.54 us -> 0.41 us  [shards(): (rows == jnp.arange(owners * signals, dtype=jnp.int32)[None, :]).astype(j...]
    unnamed x10 -> x8, local copies, waits for them, and re-layouts: 4.71 us -> 2.99 us
where the time goes in v1:
time: 114 us; the launch traced here: 112 us
  waiting for transfers between devices  70.5 us (62%)
  starting transfers between devices  27.9 us (24%)
  Pallas kernels  8.62 us (8%)
  local copies, waits for them, and re-layouts  4.06 us (4%)
  other arithmetic  1.3 us (1%)
    all_to_all x1, waiting for transfers between devices, shards(): lax.all_to_all(spectra, 'wide', split_axis=0, concat_axis=0, tiled=True)  53.8 us
    all_to_all x1, starting transfers between devices, shards(): lax.all_to_all(spectra, 'wide', split_axis=0, concat_axis=0, tiled=True)  19.3 us
    all_to_all x1, waiting for transfers between devices, shards(): lax.all_to_all(chosen, 'tm', split_axis=0, concat_axis=0, tiled=True)  14.6 us
    all_to_all x1, starting transfers between devices, shards(): lax.all_to_all(chosen, 'tm', split_axis=0, concat_axis=0, tiled=True)  5.19 us
    pallas_call x1, Pallas kernels, channelize(): pl.pallas_call(channelize_kernel, out_shape=jax.ShapeDtypeStruct((rows, s...  4.15 us
    ppermute x1, starting transfers between devices, shifted(): lax.ppermute(value, axis, [(source, source + steps) for source in range(i...  3.39 us
    unnamed x8, local copies, waits for them, and re-layouts  2.99 us
  transfers between devices with their start and end apart: 3, of which 3 were waited for; matrix products, arithmetic and copies ran while one was open for 1% of the time, Pallas kernels for 0%

profile of v1, /device:TPU:24, one launch (start us, length us, event | category | flops | bytes accessed | tf_op | source)
XLA Modules:
  0.0 112.5 jit_solution(7217157728946506895)
XLA Ops:
  0.0 0.0 copy-start.3
  0.0 0.9 slice.3
  0.9 3.4 %collective-permute-start = (bf16[2,8,2816]{2,1,0:T(8,128)(2,1)S(1)}, bf16[2,8,2816]{2,1,0:T(8,128)(2,1)S(1)}, u32[]{:S(2)}, u32[]{:S(2)}) collective-permute-start(bf16[2,8,2816]{2,1,0:T(8,128)(2,1)S(1)} %slice.3), channel_id=1, source_target_pairs={{0,1},{1,2},{2,3},{4,5},{5,6},{6,7},{8,9},{9,10},{10,11},{12,13},{... | collective-permute-start | bytes 270344 | tf_op jit(solution)/shard_map/ppermute | solution.py:19
  4.3 2.1 %collective-permute-done.halo_ref = bf16[2,8,2816]{2,1,0:T(8,128)(2,1)S(1)} collective-permute-done((bf16[2,8,2816]{2,1,0:T(8,128)(2,1)S(1)}, bf16[2,8,2816]{2,1,0:T(8,128)(2,1)S(1)}, u32[]{:S(2)}, u32[]{:S(2)}) %collective-permute-start) | collective-permute-done | bytes 90144 | tf_op jit(solution)/shard_map/ppermute | solution.py:19
  6.4 0.0 copy-start
  6.4 1.2 %copy-done = bf16[2,8,32768]{2,1,0:T(8,128)(2,1)S(1)} copy-done((bf16[2,8,32768]{2,1,0:T(8,128)(2,1)S(1)}, bf16[2,8,32768]{2,1,0:T(8,128)(2,1)}, u32[]{:S(2)}) %copy-start) | copy-done | bytes 1048600
  7.6 0.0 copy-start.1
  7.7 1.0 copy-done.1
  8.7 0.0 copy-start.2
  8.7 0.7 copy-done.2
  9.4 4.2 %channelize.1 = bf16[512,8,128]{2,1,0:T(8,128)(2,1)} custom-call(bf16[2,8,32768]{2,1,0:T(8,128)(2,1)S(1)} %copy-done, bf16[2,8,2816]{2,1,0:T(8,128)(2,1)S(1)} %collective-permute-done.halo_ref, f32[12,256]{1,0:T(8,128)S(1)} %copy-done.2, bf16[512,512]{1,0:T(8,128)(2,1)S(1)} %copy-done.1), custom_call_target="tpu_custom_call" | custom-call | flops 600000000 | bytes 3000000 | tf_op jit(solution)/shard_map/channelize/pallas_call | solution.py:92
  13.6 19.3 %all-to-all-start = ((bf16[128,4,8,128]{3,2,1,0:T(8,128)(2,1)}), bf16[128,4,8,128]{3,2,1,0:T(8,128)(2,1)S(1)}, u32[]{:S(2)}, u32[]{:S(2)}) async-start(bf16[128,4,8,128]{3,2,1,0:T(8,128)(2,1)} %bitcast.1), calls=%async_computation | async-start | bytes 2097152 | tf_op jit(solution)/shard_map/all_to_all | solution.py:168
  32.9 0.0 copy-done.3
  32.9 0.1 iota_add_fusion
  33.0 0.2 add.31
  33.2 0.4 fusion.pick_ref
  33.6 53.8 %all-to-all-done.x_ref = bf16[128,4,8,128]{3,2,1,0:T(8,128)(2,1)S(1)} async-done(((bf16[128,4,8,128]{3,2,1,0:T(8,128)(2,1)}), bf16[128,4,8,128]{3,2,1,0:T(8,128)(2,1)S(1)}, u32[]{:S(2)}, u32[]{:S(2)}) %all-to-all-start) | async-done | bytes 1048608 | tf_op jit(solution)/shard_map/all_to_all | solution.py:168
  87.4 2.2 %choose.1 = bf16[4,4,256,128]{3,2,1,0:T(8,128)(2,1)} custom-call(bf16[1024,1024]{1,0:T(8,128)(2,1)S(1)} %fusion.pick_ref, bf16[128,4,8,128]{3,2,1,0:T(8,128)(2,1)S(1)} %all-to-all-done.x_ref), custom_call_target="tpu_custom_call" | custom-call | flops 1100000000 | bytes 4000000 | tf_op jit(solution)/shard_map/choose/pallas_call | solution.py:122
  89.6 5.2 %all-to-all-start.1 = ((bf16[4,4,256,128]{3,2,1,0:T(8,128)(2,1)}), bf16[4,4,256,128]{3,2,1,0:T(8,128)(2,1)S(1)}, u32[]{:S(2)}, u32[]{:S(2)}) async-start(bf16[4,4,256,128]{3,2,1,0:T(8,128)(2,1)} %choose.1), calls=%async_computation.1 | async-start | bytes 2097152 | tf_op jit(solution)/shard_map/all_to_all | solution.py:172
  94.8 0.8 multiply_bitcast_fusion.weight_ref
  95.6 14.6 %all-to-all-done.1.x_ref = bf16[4,4,256,128]{3,2,1,0:T(8,128)(2,1)S(1)} async-done(((bf16[4,4,256,128]{3,2,1,0:T(8,128)(2,1)}), bf16[4,4,256,128]{3,2,1,0:T(8,128)(2,1)S(1)}, u32[]{:S(2)}, u32[]{:S(2)}) %all-to-all-start.1) | async-done | bytes 1048608 | tf_op jit(solution)/shard_map/all_to_all | solution.py:172
  110.2 2.2 %correlate.1 = f32[1,2,2,256,256]{4,3,2,1,0:T(8,128)} custom-call(f32[2]{0:T(128)S(1)} %multiply_bitcast_fusion.weight_ref, bf16[4,4,256,128]{3,2,1,0:T(8,128)(2,1)S(1)} %all-to-all-done.1.x_ref), custom_call_target="tpu_custom_call" | custom-call | flops 600000000 | bytes 2000000 | tf_op jit(solution)/shard_map/correlate/pallas_call | solution.py:146
  (1 shorter events, 0.0 us)
Async XLA Ops:
  0.0 32.9 %copy-start.3 = (s32[4,128]{1,0:T(4,128)S(1)}, s32[4,128]{1,0:T(4,128)}, u32[]{:S(2)}) copy-start(s32[4,128]{1,0:T(4,128)} %param.7) | copy-start | bytes 6148
  0.9 5.5 %collective-permute-start = (bf16[2,8,2816]{2,1,0:T(8,128)(2,1)S(1)}, bf16[2,8,2816]{2,1,0:T(8,128)(2,1)S(1)}, u32[]{:S(2)}, u32[]{:S(2)}) collective-permute-start(bf16[2,8,2816]{2,1,0:T(8,128)(2,1)S(1)} %slice.3), channel_id=1, source_target_pairs={{0,1},{1,2},{2,3},{4,5},{5,6},{6,7},{8,9},{9,10},{10,11},{12,13},{... | collective-permute-start | bytes 270344 | tf_op jit(solution)/shard_map/ppermute | solution.py:19
  6.4 1.2 %copy-start = (bf16[2,8,32768]{2,1,0:T(8,128)(2,1)S(1)}, bf16[2,8,32768]{2,1,0:T(8,128)(2,1)}, u32[]{:S(2)}) copy-start(bf16[2,8,32768]{2,1,0:T(8,128)(2,1)} %x_ref.1) | copy-start | bytes 3145732
  7.6 1.0 copy-start.1
  8.7 0.7 copy-start.2
  13.6 73.9 %all-to-all-start = ((bf16[128,4,8,128]{3,2,1,0:T(8,128)(2,1)}), bf16[128,4,8,128]{3,2,1,0:T(8,128)(2,1)S(1)}, u32[]{:S(2)}, u32[]{:S(2)}) async-start(bf16[128,4,8,128]{3,2,1,0:T(8,128)(2,1)} %bitcast.1), calls=%async_computation | async-start | bytes 2097152 | tf_op jit(solution)/shard_map/all_to_all | solution.py:168
  89.6 20.6 %all-to-all-start.1 = ((bf16[4,4,256,128]{3,2,1,0:T(8,128)(2,1)}), bf16[4,4,256,128]{3,2,1,0:T(8,128)(2,1)S(1)}, u32[]{:S(2)}, u32[]{:S(2)}) async-start(bf16[4,4,256,128]{3,2,1,0:T(8,128)(2,1)} %choose.1), calls=%async_computation.1 | async-start | bytes 2097152 | tf_op jit(solution)/shard_map/all_to_all | solution.py:172

commit v2 on v1

v2 whole, which is shorter than its diff:
```python
import math

import jax
import jax.numpy as jnp
import numpy as np
from jax import lax
from jax.experimental import pallas as pl
from jax.experimental.pallas import tpu as pltpu
from jax.sharding import PartitionSpec as P

LANES = 128
BLOCK = 16
WIDE_FIRST = 76
TM_FIRST = 1
IN_VMEM = pl.BlockSpec(memory_space=pltpu.VMEM)
IN_HBM = pl.BlockSpec(memory_space=pltpu.HBM)
IN_SMEM = pl.BlockSpec(memory_space=pltpu.SMEM)
PARAMS = pltpu.CompilerParams(vmem_limit_bytes=24 * 1024 * 1024)
CONTRACT_LAST = (((1,), (1,)), ((), ()))


def shifted(value, axis, steps):
    count = lax.axis_size(axis)
    initial, last = (max(0, -steps), min(count, count - steps))
    return lax.ppermute(value, axis, [(source, source + steps) for source in range(initial, last)])


def member_order(count, first):
    return [(first + step) % count for step in range(count)]


def exchange(value, axis, order):
    return lax.all_to_all(value, axis, split_axis=0, concat_axis=0, tiled=True, axis_index_groups=[order])


def transform_table(length, order):
    grid = np.arange(length)[:, None] * np.arange(length)[None, :] % length
    angle = grid * (2.0 * math.pi / length)
    scale = 1.0 / math.sqrt(length)
    cosine, sine = np.cos(angle) * scale, np.sin(angle) * scale
    real = np.concatenate([cosine, sine], axis=1)
    imaginary = np.concatenate([-sine, cosine], axis=1)
    table = np.stack([real, imaginary], axis=1).reshape(len(order), -1, 2 * length)[np.asarray(order)]
    return table.reshape(2 * length, 2 * length).astype(jnp.bfloat16)


def stage_kernel(x_ref, taps_ref, table_ref, x_out, tail_out, taps_out, table_out, sems):
    length = tail_out.shape[2]
    first = x_ref.shape[2] - length
    copies = [
        pltpu.make_async_copy(x_ref.at[:, :, first:], tail_out, sems.at[0]),
        pltpu.make_async_copy(x_ref, x_out, sems.at[1]),
        pltpu.make_async_copy(taps_ref, taps_out, sems.at[2]),
        pltpu.make_async_copy(table_ref, table_out, sems.at[3]),
    ]
    for copy in copies:
        copy.start()
    for copy in copies:
        copy.wait()


def stage(voltages, filter_taps, table):
    taps, length = filter_taps.shape
    tail = voltages.shape[:2] + ((taps - 1) * length,)
    operands = [pltpu.with_memory_space_constraint(value, pltpu.HBM) for value in (voltages, filter_taps, table)]
    return pl.pallas_call(
        stage_kernel,
        in_specs=[IN_HBM] * 3,
        out_specs=[IN_VMEM] * 4,
        out_shape=[
            pltpu.VMEM(voltages.shape, voltages.dtype),
            pltpu.VMEM(tail, voltages.dtype),
            pltpu.VMEM(filter_taps.shape, filter_taps.dtype),
            pltpu.VMEM(table.shape, table.dtype),
        ],
        scratch_shapes=[pltpu.SemaphoreType.DMA((4,))],
        compiler_params=PARAMS,
        name="stage",
    )(*operands)


def load_frame(ref, part, frame, col, cols):
    start = (frame * cols + col) * LANES
    if not isinstance(start, int):
        start = pl.multiple_of(start, LANES)
    return ref[part, :, pl.ds(start, LANES)].astype(jnp.float32)


def tap_weights(taps_ref, col, signals):
    row = [taps_ref[tap : tap + 1, col * LANES : (col + 1) * LANES] for tap in range(taps_ref.shape[0])]
    return [jnp.broadcast_to(value, (signals, LANES)) for value in row]


def filter_frame(weights, window):
    total = weights[0] * window[0]
    for weight, value in zip(weights[1:], window[1:]):
        total = total + weight * value
    return total


def filter_kernel(x_ref, taps_ref, out_ref):
    taps, length = taps_ref.shape
    signals = x_ref.shape[1]
    cols = length // LANES
    frames = x_ref.shape[2] // length
    for part in range(2):
        for col in range(cols):
            weights = tap_weights(taps_ref, col, signals)

            def step(block, window, part=part, col=col, weights=weights):
                first = block * BLOCK
                window = list(window) + [
                    load_frame(x_ref, part, first + frame, col, cols) for frame in range(BLOCK)
                ]
                for frame in range(BLOCK):
                    total = filter_frame(weights, window[frame : frame + taps])
                    out_ref[part, col, pl.ds(first + frame, signals, stride=frames), :] = total
                return tuple(window[BLOCK:])

            opening = tuple(
                load_frame(x_ref, part, BLOCK - (taps - 1) + frame, col, cols) for frame in range(taps - 1)
            )
            lax.fori_loop(1, frames // BLOCK, step, opening, unroll=frames // BLOCK - 1)


def filter_body(x, filter_taps):
    _, signals, samples = x.shape
    length = filter_taps.shape[1]
    shape = (2, length // LANES, signals * (samples // length), LANES)
    return pl.pallas_call(
        filter_kernel,
        in_specs=[IN_VMEM] * 2,
        out_specs=IN_VMEM,
        out_shape=pltpu.VMEM(shape, jnp.float32),
        compiler_params=PARAMS,
        cost_estimate=pl.CostEstimate(flops=12_000_000, bytes_accessed=6_000_000, transcendentals=0),
        name="filter_body",
    )(x, filter_taps)


def transform_kernel(body_ref, halo_ref, x_ref, taps_ref, table_ref, out_ref, opening, turned):
    taps, length = taps_ref.shape
    signals = x_ref.shape[1]
    cols = length // LANES
    frames = x_ref.shape[2] // length
    for part in range(2):
        for col in range(cols):
            weights = tap_weights(taps_ref, col, signals)
            window = [load_frame(halo_ref, part, frame, col, cols) for frame in range(taps - 1)]
            window += [load_frame(x_ref, part, frame, col, cols) for frame in range(BLOCK)]
            for frame in range(BLOCK):
                total = filter_frame(weights, window[frame : frame + taps])
                opening[part, col, pl.ds(frame, signals, stride=BLOCK), :] = total

    rows = table_ref.shape[0]
    for pair in range(0, signals, 2):
        columns = []
        for part in range(2):
            for col in range(cols):
                pieces = []
                for signal in (pair, pair + 1):
                    pieces.append(opening[part, col, signal * BLOCK : (signal + 1) * BLOCK, :])
                    pieces.append(body_ref[part, col, signal * frames + BLOCK : (signal + 1) * frames, :])
                columns.append(jnp.concatenate(pieces, axis=0))
        samples = jnp.concatenate(columns, axis=1).astype(jnp.bfloat16)
        spectrum = lax.dot_general(table_ref[...], samples, CONTRACT_LAST, preferred_element_type=jnp.float32)
        for which in range(2):
            turned[pl.ds(pair + which, rows, stride=signals), :] = spectrum[
                :, which * frames : (which + 1) * frames
            ]
    out_ref[...] = turned[...].astype(jnp.bfloat16).reshape(out_ref.shape)


def transform(body, halo, x, filter_taps, table):
    taps, length = filter_taps.shape
    signals = x.shape[1]
    frames = x.shape[2] // length
    rows = table.shape[0]
    return pl.pallas_call(
        transform_kernel,
        in_specs=[IN_VMEM] * 5,
        out_specs=IN_VMEM,
        out_shape=pltpu.VMEM((rows, signals, frames), jnp.bfloat16),
        scratch_shapes=[
            pltpu.VMEM((2, length // LANES, signals * BLOCK, LANES), jnp.float32),
            pltpu.VMEM((rows * signals, frames), jnp.float32),
        ],
        compiler_params=PARAMS,
        cost_estimate=pl.CostEstimate(flops=540_000_000, bytes_accessed=4_000_000, transcendentals=0),
        name="transform",
    )(body, halo, x, filter_taps, table)


def choose_kernel(rows_ref, signal_ref, x_ref, out_ref):
    sources, parts, signals, frames = x_ref.shape
    subs, _, members, _ = out_ref.shape
    columns = jnp.concatenate(
        [x_ref[:, part].reshape(sources * signals, frames) for part in range(parts)], axis=1
    )
    held = signal_ref[...]
    for sub in range(subs):
        wanted = rows_ref[sub * members : (sub + 1) * members, :]
        pick = jnp.where(wanted == held, 1.0, 0.0).astype(jnp.bfloat16)
        chosen = jnp.dot(pick, columns, preferred_element_type=jnp.float32).astype(jnp.bfloat16)
        for part in range(parts):
            out_ref[sub, part] = chosen[:, part * frames : (part + 1) * frames]


def choose(rows, held, turned, subs):
    _, parts, _, frames = turned.shape
    return pl.pallas_call(
        choose_kernel,
        in_specs=[IN_VMEM] * 3,
        out_specs=IN_VMEM,
        out_shape=pltpu.VMEM((subs, parts, rows.shape[0] // subs, frames), jnp.bfloat16),
        compiler_params=PARAMS,
        cost_estimate=pl.CostEstimate(flops=1_100_000_000, bytes_accessed=2_000_000, transcendentals=0),
        name="choose",
    )(rows, held, turned)


def correlate_kernel(weight_ref, x_ref, out_ref, grams, sems):
    segments = x_ref.shape[0]
    copies = []
    for channel in range(out_ref.shape[1]):
        real = [x_ref[segment, 2 * channel] for segment in range(segments)]
        imag = [x_ref[segment, 2 * channel + 1] for segment in range(segments)]
        left = jnp.concatenate(real + imag, axis=1)
        turned = jnp.concatenate(imag + [-value for value in real], axis=1)
        weight = weight_ref[channel]
        for part, rows in enumerate((left, turned)):
            grams[channel, part] = weight * lax.dot_general(
                rows, left, CONTRACT_LAST, preferred_element_type=jnp.float32
            )
            copy = pltpu.make_async_copy(
                grams.at[channel, part], out_ref.at[0, channel, part], sems.at[2 * channel + part]
            )
            copy.start()
            copies.append(copy)
    for copy in copies:
        copy.wait()


def correlate(weights, gathered):
    _, parts, members, _ = gathered.shape
    shape = (parts // 2, 2, members, members)
    return pl.pallas_call(
        correlate_kernel,
        in_specs=[IN_SMEM, IN_VMEM],
        out_specs=IN_HBM,
        out_shape=jax.ShapeDtypeStruct((1,) + shape, jnp.float32),
        scratch_shapes=[pltpu.VMEM(shape, jnp.float32), pltpu.SemaphoreType.DMA((parts,))],
        compiler_params=PARAMS,
        cost_estimate=pl.CostEstimate(flops=540_000_000, bytes_accessed=2_000_000, transcendentals=0),
        name="correlate",
    )(weights, gathered)


def shards(voltages, filter_taps, stations, allocation):
    length = filter_taps.shape[1]
    signals = voltages.shape[1]
    frames = voltages.shape[2] // length
    segments = lax.axis_size("tm")
    owners = lax.axis_size("wide")
    sub = lax.axis_index("tm")
    num_subs = stations.shape[0]
    ch_dev = length // owners
    wide_order = member_order(owners, WIDE_FIRST % owners)
    tm_order = member_order(segments, TM_FIRST % segments)

    table = jnp.asarray(transform_table(length, wide_order))
    x, tail, taps, table = stage(voltages, filter_taps, table)
    halo = shifted(tail, "tm", 1)
    body = filter_body(x, taps)
    spectra = transform(body, halo, x, taps, table)
    turned = exchange(spectra.reshape(owners, 2 * ch_dev, signals, frames), "wide", wide_order)

    by_owner = jnp.concatenate([stations[which : which + 1] for which in tm_order], axis=0)
    rows = (2 * by_owner[:, :, None] + jnp.arange(2, dtype=jnp.int32)[None, None, :]).reshape(-1, 1)
    held = np.asarray(wide_order)[:, None] * signals + np.arange(signals)[None, :]
    held = jnp.asarray(held.reshape(1, -1), jnp.int32)
    mine = lax.dynamic_slice(allocation, (sub, lax.axis_index("wide") * ch_dev), (1, ch_dev)).reshape(ch_dev)
    weights = mine.astype(jnp.float32) * (1.0 / (frames * segments))

    chosen = choose(rows, held, turned, num_subs)
    return correlate(weights, exchange(chosen, "tm", tm_order))


def solution(mesh):
    return jax.shard_map(
        shards,
        mesh=mesh,
        in_specs=(P(None, "wide", "tm"), P(), P(), P()),
        out_specs=P("tm", "wide", None, None, None),
        check_vma=False,
    )
```

time: 114 us -> 103 us (0.904)
  waiting for transfers between devices: 70.5 us -> 61.2 us
  local copies, waits for them, and re-layouts: 4.06 us -> 0.16 us
  starting transfers between devices: 27.9 us -> 29.9 us
    all_to_all x2, waiting for transfers between devices: 68.4 us -> 60.7 us  [exchange(): lax.all_to_all(value, axis, split_axis=0, concat_axis=0, tiled=True, axis...]
    unnamed x8 -> x4, local copies, waits for them, and re-layouts: 2.99 us -> 0.01 us
    all_to_all x2, starting transfers between devices: 24.5 us -> 26.5 us  [exchange(): lax.all_to_all(value, axis, split_axis=0, concat_axis=0, tiled=True, axis...]
    ppermute x1, waiting for transfers between devices: 2.11 us -> 0.5 us  [shifted(): lax.ppermute(value, axis, [(source, source + steps) for source in range(i...]
    pallas_call x3 -> x5, Pallas kernels: 8.62 us -> 9.46 us  [the longest x1 2.27 us: choose(): pl.pallas_call(choose_kernel, in_specs=[IN_VMEM] * 3, out_specs=IN_VMEM,...]
  transfers between devices with their start and end apart: 3 -> 3, of which waited for: 3 -> 3; matrix products, arithmetic and copies ran while one was open for 1% -> 1% of each run, Pallas kernels for 0% -> 2%
where the time goes in v2:
time: 103 us; the launch traced here: 102 us
  waiting for transfers between devices  61.2 us (59%)
  starting transfers between devices  29.9 us (29%)
  Pallas kernels  9.46 us (9%)
    all_to_all x2, waiting for transfers between devices, exchange(): lax.all_to_all(value, axis, split_axis=0, concat_axis=0, tiled=True, axis...  60.7 us
    all_to_all x2, starting transfers between devices, exchange(): lax.all_to_all(value, axis, split_axis=0, concat_axis=0, tiled=True, axis...  26.5 us
    ppermute x1, starting transfers between devices, shifted(): lax.ppermute(value, axis, [(source, source + steps) for source in range(i...  3.4 us
    pallas_call x1, Pallas kernels, choose(): pl.pallas_call(choose_kernel, in_specs=[IN_VMEM] * 3, out_specs=IN_VMEM,...  2.27 us
    pallas_call x1, Pallas kernels, correlate(): pl.pallas_call(correlate_kernel, in_specs=[IN_SMEM, IN_VMEM], out_specs=I...  2.11 us
  transfers between devices with their start and end apart: 3, of which 3 were waited for; matrix products, arithmetic and copies ran while one was open for 1% of the time, Pallas kernels for 2%

profile of v2, /device:TPU:24, one launch (start us, length us, event | category | flops | bytes accessed | tf_op | source)
XLA Modules:
  0.0 101.6 jit_solution(6294447743043483337)
XLA Ops:
  0.0 1.5 %stage.1 = (bf16[2,8,32768]{2,1,0:T(8,128)(2,1)S(1)}, bf16[2,8,2816]{2,1,0:T(8,128)(2,1)S(1)}, f32[12,256]{1,0:T(8,128)S(1)}, bf16[512,512]{1,0:T(8,128)(2,1)S(1)}) custom-call(bf16[2,8,32768]{2,1,0:T(8,128)(2,1)} %x_ref.1, f32[12,256]{1,0:T(8,128)} %taps_ref.1, bf16[512,512]{1,0:T(8,128)(2,1)} %constant.24.clone.table_ref), custom_call_target="tpu_custom_call" | custom-call | tf_op jit(solution)/shard_map/stage/pallas_call | solution.py:66
  1.5 3.4 %collective-permute-start = (bf16[2,8,2816]{2,1,0:T(8,128)(2,1)S(1)}, bf16[2,8,2816]{2,1,0:T(8,128)(2,1)S(1)}, u32[]{:S(2)}, u32[]{:S(2)}) collective-permute-start(bf16[2,8,2816]{2,1,0:T(8,128)(2,1)S(1)} %get-tuple-element.11), channel_id=1, source_target_pairs={{0,1},{1,2},{2,3},{4,5},{5,6},{6,7},{8,9},{9,10},{10,11},{12,13},{... | collective-permute-start | bytes 270344 | tf_op jit(solution)/shard_map/ppermute | solution.py:25
  4.9 1.6 %filter_body.1.body_ref = f32[2,2,1024,128]{3,2,1,0:T(8,128)S(1)} custom-call(bf16[2,8,32768]{2,1,0:T(8,128)(2,1)S(1)} %get-tuple-element.9.x_ref, f32[12,256]{1,0:T(8,128)S(1)} %get-tuple-element.10.taps_ref), custom_call_target="tpu_custom_call" | custom-call | flops 12000000 | bytes 6000000 | tf_op jit(solution)/shard_map/filter_body/pallas_call | solution.py:130
  6.5 0.5 collective-permute-done.halo_ref
  7.0 2.0 %transform.1 = bf16[512,8,128]{2,1,0:T(8,128)(2,1)} custom-call(f32[2,2,1024,128]{3,2,1,0:T(8,128)S(1)} %filter_body.1.body_ref, bf16[2,8,2816]{2,1,0:T(8,128)(2,1)S(1)} %collective-permute-done.halo_ref, bf16[2,8,32768]{2,1,0:T(8,128)(2,1)S(1)} %get-tuple-element.9.x_ref, f32[12,256]{1,0:T(8,128)S(1)} %get-tuple-element.10.taps_ref, ...), custom_call_target="tpu_custom_call" | custom-call | flops 540000000 | bytes 4000000 | tf_op jit(solution)/shard_map/transform/pallas_call | solution.py:179
  9.0 0.0 copy-start.1
  9.0 0.0 slice-start
  9.0 0.0 copy-start
  9.0 20.6 %all-to-all-start = ((bf16[128,4,8,128]{3,2,1,0:T(8,128)(2,1)}), bf16[128,4,8,128]{3,2,1,0:T(8,128)(2,1)S(1)}, u32[]{:S(2)}, u32[]{:S(2)}) async-start(bf16[128,4,8,128]{3,2,1,0:T(8,128)(2,1)} %bitcast.1), calls=%async_computation | async-start | bytes 2097152 | tf_op jit(solution)/shard_map/all_to_all | solution.py:33
  29.6 0.0 copy-done.1
  29.6 0.0 slice-done
  29.6 0.1 iota_add_fusion
  29.8 0.1 add.35.rows_ref
  29.9 47.3 %all-to-all-done.x_ref = bf16[128,4,8,128]{3,2,1,0:T(8,128)(2,1)S(1)} async-done(((bf16[128,4,8,128]{3,2,1,0:T(8,128)(2,1)}), bf16[128,4,8,128]{3,2,1,0:T(8,128)(2,1)S(1)}, u32[]{:S(2)}, u32[]{:S(2)}) %all-to-all-start) | async-done | bytes 1048608 | tf_op jit(solution)/shard_map/all_to_all | solution.py:33
  77.3 0.0 copy-done
  77.3 2.3 %choose.1 = bf16[4,4,256,128]{3,2,1,0:T(8,128)(2,1)} custom-call(s32[1024,1]{1,0:T(8,128)S(1)} %add.35.rows_ref, s32[1,1024]{1,0:T(1,128)S(1)} %copy-done, bf16[128,4,8,128]{3,2,1,0:T(8,128)(2,1)S(1)} %all-to-all-done.x_ref), custom_call_target="tpu_custom_call" | custom-call | flops 1100000000 | bytes 2000000 | tf_op jit(solution)/shard_map/choose/pallas_call | solution.py:211
  79.6 5.9 %all-to-all-start.1 = ((bf16[4,4,256,128]{3,2,1,0:T(8,128)(2,1)}), bf16[4,4,256,128]{3,2,1,0:T(8,128)(2,1)S(1)}, u32[]{:S(2)}, u32[]{:S(2)}) async-start(bf16[4,4,256,128]{3,2,1,0:T(8,128)(2,1)} %choose.1), calls=%async_computation.1 | async-start | bytes 2097152 | tf_op jit(solution)/shard_map/all_to_all | solution.py:33
  85.4 0.8 multiply_bitcast_fusion.weight_ref
  86.2 13.3 %all-to-all-done.1.x_ref = bf16[4,4,256,128]{3,2,1,0:T(8,128)(2,1)S(1)} async-done(((bf16[4,4,256,128]{3,2,1,0:T(8,128)(2,1)}), bf16[4,4,256,128]{3,2,1,0:T(8,128)(2,1)S(1)}, u32[]{:S(2)}, u32[]{:S(2)}) %all-to-all-start.1) | async-done | bytes 1048608 | tf_op jit(solution)/shard_map/all_to_all | solution.py:33
  99.5 2.1 %correlate.1 = f32[1,2,2,256,256]{4,3,2,1,0:T(8,128)} custom-call(f32[2]{0:T(128)S(1)} %multiply_bitcast_fusion.weight_ref, bf16[4,4,256,128]{3,2,1,0:T(8,128)(2,1)S(1)} %all-to-all-done.1.x_ref), custom_call_target="tpu_custom_call" | custom-call | flops 540000000 | bytes 2000000 | tf_op jit(solution)/shard_map/correlate/pallas_call | solution.py:247
  (2 shorter events, 0.0 us)
Async XLA Ops:
  1.5 5.5 %collective-permute-start = (bf16[2,8,2816]{2,1,0:T(8,128)(2,1)S(1)}, bf16[2,8,2816]{2,1,0:T(8,128)(2,1)S(1)}, u32[]{:S(2)}, u32[]{:S(2)}) collective-permute-start(bf16[2,8,2816]{2,1,0:T(8,128)(2,1)S(1)} %get-tuple-element.11), channel_id=1, source_target_pairs={{0,1},{1,2},{2,3},{4,5},{5,6},{6,7},{8,9},{9,10},{10,11},{12,13},{... | collective-permute-start | bytes 270344 | tf_op jit(solution)/shard_map/ppermute | solution.py:25
  9.0 20.6 %copy-start.1 = (s32[4,128]{1,0:T(4,128)S(1)}, s32[4,128]{1,0:T(4,128)}, u32[]{:S(2)}) copy-start(s32[4,128]{1,0:T(4,128)} %param.8) | copy-start | bytes 6148
  9.0 20.6 %slice-start = ((s32[4,128]{1,0:T(4,128)}), s32[1,128]{1,0:T(1,128)S(1)}, s32[]{:S(2)}) async-start(s32[4,128]{1,0:T(4,128)} %param.8), calls=%async_computation.2 | async-start | bytes 1024 | tf_op jit(solution)/shard_map/slice | solution.py:278
  9.0 68.3 %copy-start = (s32[1,1024]{1,0:T(1,128)S(1)}, s32[1,1024]{1,0:T(1,128)}, u32[]{:S(2)}) copy-start(s32[1,1024]{1,0:T(1,128)} %constant.25.clone.signal_ref) | copy-start | bytes 12292
  9.0 68.3 %all-to-all-start = ((bf16[128,4,8,128]{3,2,1,0:T(8,128)(2,1)}), bf16[128,4,8,128]{3,2,1,0:T(8,128)(2,1)S(1)}, u32[]{:S(2)}, u32[]{:S(2)}) async-start(bf16[128,4,8,128]{3,2,1,0:T(8,128)(2,1)} %bitcast.1), calls=%async_computation | async-start | bytes 2097152 | tf_op jit(solution)/shard_map/all_to_all | solution.py:33
  79.6 20.0 %all-to-all-start.1 = ((bf16[4,4,256,128]{3,2,1,0:T(8,128)(2,1)}), bf16[4,4,256,128]{3,2,1,0:T(8,128)(2,1)S(1)}, u32[]{:S(2)}, u32[]{:S(2)}) async-start(bf16[4,4,256,128]{3,2,1,0:T(8,128)(2,1)} %choose.1), calls=%async_computation.1 | async-start | bytes 2097152 | tf_op jit(solution)/shard_map/all_to_all | solution.py:33

commit v3 on v2

--- a/solution.py
+++ b/solution.py
@@ -44,39 +44,31 @@
     return table.reshape(2 * length, 2 * length).astype(jnp.bfloat16)
 
 
-def stage_kernel(x_ref, taps_ref, table_ref, x_out, tail_out, taps_out, table_out, sems):
-    length = tail_out.shape[2]
-    first = x_ref.shape[2] - length
-    copies = [
-        pltpu.make_async_copy(x_ref.at[:, :, first:], tail_out, sems.at[0]),
-        pltpu.make_async_copy(x_ref, x_out, sems.at[1]),
-        pltpu.make_async_copy(taps_ref, taps_out, sems.at[2]),
-        pltpu.make_async_copy(table_ref, table_out, sems.at[3]),
-    ]
+def stage_kernel(x_ref, *refs):
+    count = len(refs) // 2
+    sources, tail_out, targets, sems = refs[: count - 1], refs[count - 1], refs[count:-1], refs[-1]
+    first = x_ref.shape[2] - tail_out.shape[2]
+    copies = [pltpu.make_async_copy(x_ref.at[:, :, first:], tail_out, sems.at[0])]
+    for place, (source, target) in enumerate(zip((x_ref,) + sources, targets)):
+        copies.append(pltpu.make_async_copy(source, target, sems.at[place + 1]))
     for copy in copies:
         copy.start()
     for copy in copies:
         copy.wait()
 
 
-def stage(voltages, filter_taps, table):
-    taps, length = filter_taps.shape
-    tail = voltages.shape[:2] + ((taps - 1) * length,)
-    operands = [pltpu.with_memory_space_constraint(value, pltpu.HBM) for value in (voltages, filter_taps, table)]
+def stage(tail_length, *operands):
+    tail = operands[0].shape[:2] + (tail_length,)
     return pl.pallas_call(
         stage_kernel,
-        in_specs=[IN_HBM] * 3,
-        out_specs=[IN_VMEM] * 4,
-        out_shape=[
-            pltpu.VMEM(voltages.shape, voltages.dtype),
-            pltpu.VMEM(tail, voltages.dtype),
-            pltpu.VMEM(filter_taps.shape, filter_taps.dtype),
-            pltpu.VMEM(table.shape, table.dtype),
-        ],
-        scratch_shapes=[pltpu.SemaphoreType.DMA((4,))],
+        in_specs=[IN_HBM] * len(operands),
+        out_specs=[IN_VMEM] * (len(operands) + 1),
+        out_shape=[pltpu.VMEM(tail, operands[0].dtype)]
+        + [pltpu.VMEM(value.shape, value.dtype) for value in operands],
+        scratch_shapes=[pltpu.SemaphoreType.DMA((len(operands) + 1,))],
         compiler_params=PARAMS,
         name="stage",
-    )(*operands)
+    )(*[pltpu.with_memory_space_constraint(value, pltpu.HBM) for value in operands])
 
 
 def load_frame(ref, part, frame, col, cols):
@@ -98,7 +90,19 @@
     return total
 
 
-def filter_kernel(x_ref, taps_ref, out_ref):
+def place_rows(stations_ref, places_ref, order, first, total):
+    members = stations_ref.shape[1]
+    for block, sub in enumerate(order):
+        line = stations_ref[sub : sub + 1, :].astype(jnp.float32)
+        station = jnp.broadcast_to(line, (members, members)).T.astype(jnp.int32)
+        for pol in range(2):
+            place = 2 * station + (pol - first)
+            place = jnp.where(place < 0, place + total, place)
+            places_ref[pl.ds(block * 2 * members + pol, members, stride=2), :] = place
+
+
+def filter_kernel(x_ref, taps_ref, stations_ref, out_ref, places_ref, *, order, first, total):
+    place_rows(stations_ref, places_ref, order, first, total)
     taps, length = taps_ref.shape
     signals = x_ref.shape[1]
     cols = length // LANES
@@ -123,19 +127,20 @@
             lax.fori_loop(1, frames // BLOCK, step, opening, unroll=frames // BLOCK - 1)
 
 
-def filter_body(x, filter_taps):
+def filter_body(x, filter_taps, stations, **places):
     _, signals, samples = x.shape
     length = filter_taps.shape[1]
+    members = stations.shape[1]
     shape = (2, length // LANES, signals * (samples // length), LANES)
     return pl.pallas_call(
-        filter_kernel,
-        in_specs=[IN_VMEM] * 2,
-        out_specs=IN_VMEM,
-        out_shape=pltpu.VMEM(shape, jnp.float32),
+        lambda *refs: filter_kernel(*refs, **places),
+        in_specs=[IN_VMEM] * 3,
+        out_specs=[IN_VMEM] * 2,
+        out_shape=[pltpu.VMEM(shape, jnp.float32), pltpu.VMEM((2 * stations.size, members), jnp.int32)],
         compiler_params=PARAMS,
         cost_estimate=pl.CostEstimate(flops=12_000_000, bytes_accessed=6_000_000, transcendentals=0),
         name="filter_body",
-    )(x, filter_taps)
+    )(x, filter_taps, stations)
 
 
 def transform_kernel(body_ref, halo_ref, x_ref, taps_ref, table_ref, out_ref, opening, turned):
@@ -191,43 +196,54 @@
     )(body, halo, x, filter_taps, table)
 
 
-def choose_kernel(rows_ref, signal_ref, x_ref, out_ref):
+def choose_kernel(places_ref, x_ref, out_ref):
     sources, parts, signals, frames = x_ref.shape
     subs, _, members, _ = out_ref.shape
+    width = places_ref.shape[1]
     columns = jnp.concatenate(
         [x_ref[:, part].reshape(sources * signals, frames) for part in range(parts)], axis=1
     )
-    held = signal_ref[...]
+    lane = lax.broadcasted_iota(jnp.int32, (members, width), 1)
     for sub in range(subs):
-        wanted = rows_ref[sub * members : (sub + 1) * members, :]
-        pick = jnp.where(wanted == held, 1.0, 0.0).astype(jnp.bfloat16)
+        wanted = places_ref[sub * members : (sub + 1) * members, :]
+        pick = jnp.concatenate(
+            [
+                jnp.where(wanted == lane + start, 1.0, 0.0).astype(jnp.bfloat16)
+                for start in range(0, sources * signals, width)
+            ],
+            axis=1,
+        )
         chosen = jnp.dot(pick, columns, preferred_element_type=jnp.float32).astype(jnp.bfloat16)
         for part in range(parts):
             out_ref[sub, part] = chosen[:, part * frames : (part + 1) * frames]
 
 
-def choose(rows, held, turned, subs):
+def choose(places, turned, subs):
     _, parts, _, frames = turned.shape
     return pl.pallas_call(
         choose_kernel,
-        in_specs=[IN_VMEM] * 3,
+        in_specs=[IN_VMEM] * 2,
         out_specs=IN_VMEM,
-        out_shape=pltpu.VMEM((subs, parts, rows.shape[0] // subs, frames), jnp.bfloat16),
+        out_shape=pltpu.VMEM((subs, parts, places.shape[0] // subs, frames), jnp.bfloat16),
         compiler_params=PARAMS,
         cost_estimate=pl.CostEstimate(flops=1_100_000_000, bytes_accessed=2_000_000, transcendentals=0),
         name="choose",
-    )(rows, held, turned)
-
-
-def correlate_kernel(weight_ref, x_ref, out_ref, grams, sems):
-    segments = x_ref.shape[0]
+    )(places, turned)
+
+
+def correlate_kernel(allocation_ref, x_ref, out_ref, grams, sems):
+    segments, parts, _, frames = x_ref.shape
+    channels = parts // 2
+    first = lax.axis_index("wide") * channels
+    row = allocation_ref[pl.ds(lax.axis_index("tm"), 1), :].astype(jnp.float32) * (1.0 / (frames * segments))
+    lane = lax.broadcasted_iota(jnp.int32, row.shape, 1)
     copies = []
-    for channel in range(out_ref.shape[1]):
+    for channel in range(channels):
         real = [x_ref[segment, 2 * channel] for segment in range(segments)]
         imag = [x_ref[segment, 2 * channel + 1] for segment in range(segments)]
         left = jnp.concatenate(real + imag, axis=1)
         turned = jnp.concatenate(imag + [-value for value in real], axis=1)
-        weight = weight_ref[channel]
+        weight = jnp.sum(jnp.where(lane == first + channel, row, 0.0), axis=1, keepdims=True)
         for part, rows in enumerate((left, turned)):
             grams[channel, part] = weight * lax.dot_general(
                 rows, left, CONTRACT_LAST, preferred_element_type=jnp.float32
@@ -241,49 +257,42 @@
         copy.wait()
 
 
-def correlate(weights, gathered):
+def correlate(allocation, gathered):
     _, parts, members, _ = gathered.shape
     shape = (parts // 2, 2, members, members)
     return pl.pallas_call(
         correlate_kernel,
-        in_specs=[IN_SMEM, IN_VMEM],
+        in_specs=[IN_VMEM, IN_VMEM],
         out_specs=IN_HBM,
         out_shape=jax.ShapeDtypeStruct((1,) + shape, jnp.float32),
         scratch_shapes=[pltpu.VMEM(shape, jnp.float32), pltpu.SemaphoreType.DMA((parts,))],
         compiler_params=PARAMS,
         cost_estimate=pl.CostEstimate(flops=540_000_000, bytes_accessed=2_000_000, transcendentals=0),
         name="correlate",
-    )(weights, gathered)
+    )(allocation, gathered)
 
 
 def shards(voltages, filter_taps, stations, allocation):
-    length = filter_taps.shape[1]
+    num_taps, length = filter_taps.shape
     signals = voltages.shape[1]
     frames = voltages.shape[2] // length
-    segments = lax.axis_size("tm")
     owners = lax.axis_size("wide")
-    sub = lax.axis_index("tm")
-    num_subs = stations.shape[0]
-    ch_dev = length // owners
     wide_order = member_order(owners, WIDE_FIRST % owners)
-    tm_order = member_order(segments, TM_FIRST % segments)
+    tm_order = member_order(lax.axis_size("tm"), TM_FIRST % lax.axis_size("tm"))
 
     table = jnp.asarray(transform_table(length, wide_order))
-    x, tail, taps, table = stage(voltages, filter_taps, table)
+    tail, x, taps, table, stations, allocation = stage(
+        (num_taps - 1) * length, voltages, filter_taps, table, stations, allocation
+    )
     halo = shifted(tail, "tm", 1)
-    body = filter_body(x, taps)
+    body, places = filter_body(
+        x, taps, stations, order=tm_order, first=wide_order[0] * signals, total=owners * signals
+    )
     spectra = transform(body, halo, x, taps, table)
-    turned = exchange(spectra.reshape(owners, 2 * ch_dev, signals, frames), "wide", wide_order)
-
-    by_owner = jnp.concatenate([stations[which : which + 1] for which in tm_order], axis=0)
-    rows = (2 * by_owner[:, :, None] + jnp.arange(2, dtype=jnp.int32)[None, None, :]).reshape(-1, 1)
-    held = np.asarray(wide_order)[:, None] * signals + np.arange(signals)[None, :]
-    held = jnp.asarray(held.reshape(1, -1), jnp.int32)
-    mine = lax.dynamic_slice(allocation, (sub, lax.axis_index("wide") * ch_dev), (1, ch_dev)).reshape(ch_dev)
-    weights = mine.astype(jnp.float32) * (1.0 / (frames * segments))
-
-    chosen = choose(rows, held, turned, num_subs)
-    return correlate(weights, exchange(chosen, "tm", tm_order))
+    spectra = spectra.reshape(owners, 2 * length // owners, signals, frames)
+    turned = exchange(spectra, "wide", wide_order)
+    chosen = choose(places, turned, stations.shape[0])
+    return correlate(allocation, exchange(chosen, "tm", tm_order))
 
 
 def solution(mesh):

time: 103 us -> 99.2 us (0.963)
  blocking collectives: 0 us -> 87.1 us
  waiting for transfers between devices: 61.2 us -> 0.31 us
  starting transfers between devices: 29.9 us -> 3.4 us
  Pallas kernels: 9.46 us -> 7.14 us
    all_to_all x0 -> x2, blocking collectives: none -> 87.1 us  [exchange(): lax.all_to_all(value, axis, split_axis=0, concat_axis=0, tiled=True, axis...]
    all_to_all x2 -> x0, waiting for transfers between devices: 60.7 us -> none  [exchange(): lax.all_to_all(value, axis, split_axis=0, concat_axis=0, tiled=True, axis...]
    all_to_all x2 -> x0, starting transfers between devices: 26.5 us -> none  [exchange(): lax.all_to_all(value, axis, split_axis=0, concat_axis=0, tiled=True, axis...]
    pallas_call x4, Pallas kernels: 7.45 us -> 6.09 us  [the longest x1 1.79 us: filter_body(): pl.pallas_call(lambda *refs: filter_kernel(*refs, **places), in_specs=[IN...]
  transfers between devices with their start and end apart: 3 -> 1, of which waited for: 3 -> 1; matrix products, arithmetic and copies ran while one was open for 1% -> 0% of each run, Pallas kernels for 2% -> 2%
where the time goes in v3:
time: 99.2 us; the launch traced here: 98 us
  blocking collectives  87.1 us (88%)
  Pallas kernels  7.14 us (7%)
  starting transfers between devices  3.4 us (3%)
    all_to_all x2, blocking collectives, exchange(): lax.all_to_all(value, axis, split_axis=0, concat_axis=0, tiled=True, axis...  87.1 us
    ppermute x1, starting transfers between devices, shifted(): lax.ppermute(value, axis, [(source, source + steps) for source in range(i...  3.4 us
  transfers between devices with their start and end apart: 1, of which 1 were waited for; matrix products, arithmetic and copies ran while one was open for 0% of the time, Pallas kernels for 2%

profile of v3, /device:TPU:24, one launch (start us, length us, event | category | flops | bytes accessed | tf_op | source)
XLA Modules:
  0.0 98.0 jit_solution(2434376432665794816)
XLA Ops:
  0.0 1.5 %stage.1 = (bf16[2,8,2816]{2,1,0:T(8,128)(2,1)S(1)}, bf16[2,8,32768]{2,1,0:T(8,128)(2,1)S(1)}, f32[12,256]{1,0:T(8,128)S(1)}, bf16[512,512]{1,0:T(8,128)(2,1)S(1...) custom-call(bf16[2,8,32768]{2,1,0:T(8,128)(2,1)} %x_ref.1, f32[12,256]{1,0:T(8,128)} %refs_0_.1, ...), custom_call_target="tpu_custom_call" | custom-call | tf_op jit(solution)/shard_map/stage/pallas_call | solution.py:62
  1.5 3.4 %collective-permute-start = (bf16[2,8,2816]{2,1,0:T(8,128)(2,1)S(1)}, bf16[2,8,2816]{2,1,0:T(8,128)(2,1)S(1)}, u32[]{:S(2)}, u32[]{:S(2)}) collective-permute-start(bf16[2,8,2816]{2,1,0:T(8,128)(2,1)S(1)} %get-tuple-element.19), channel_id=1, source_target_pairs={{0,1},{1,2},{2,3},{4,5},{5,6},{6,7},{8,9},{9,10},{10,11},{12,13},{... | collective-permute-start | bytes 270344 | tf_op jit(solution)/shard_map/ppermute | solution.py:25
  4.9 1.8 %filter_body.1 = (f32[2,2,1024,128]{3,2,1,0:T(8,128)S(1)}, s32[1024,128]{1,0:T(8,128)S(1)}) custom-call(bf16[2,8,32768]{2,1,0:T(8,128)(2,1)S(1)} %get-tuple-element.14.refs_0_.x_ref, f32[12,256]{1,0:T(8,128)S(1)} %get-tuple-element.15.refs_1_.taps_ref, s32[4,128]{1,0:T(4,128)S(1)} %get-tuple-element.16.refs_2_), custom_call_target="tpu_custom_call" | custom-call | flops 12000000 | bytes 6000000 | tf_op jit(solution)/shard_map/filter_body/pallas_call | solution.py:135
  6.7 0.3 collective-permute-done.halo_ref
  7.0 1.0 %transform.1 = bf16[512,8,128]{2,1,0:T(8,128)(2,1)S(1)} custom-call(f32[2,2,1024,128]{3,2,1,0:T(8,128)S(1)} %get-tuple-element.18.body_ref, bf16[2,8,2816]{2,1,0:T(8,128)(2,1)S(1)} %collective-permute-done.halo_ref, bf16[2,8,32768]{2,1,0:T(8,128)(2,1)S(1)} %get-tuple-element.14.refs_0_.x_ref, f32[12,256]{1,0:T(8,128)S(1)} %get-tuple-element.15.refs_1_.taps_ref, ...), custom_call_target="tpu_custom_call" | custom-call | flops 540000000 | bytes 4000000 | tf_op jit(solution)/shard_map/transform/pallas_call | solution.py:184
  8.1 67.9 %all_to_all.10.x_ref = bf16[128,4,8,128]{3,2,1,0:T(8,128)(2,1)S(1)} all-to-all(bf16[128,4,8,128]{3,2,1,0:T(8,128)(2,1)S(1)} %bitcast.1), channel_id=1, replica_groups={{304,308,312,316,320,324,328,332,336,340,344,348,352,356,360,364,368,37..., dimensions={0} | all-to-all | bytes 2097152 | tf_op jit(solution)/shard_map/all_to_all | solution.py:33
  76.0 1.2 %choose.1 = bf16[4,4,256,128]{3,2,1,0:T(8,128)(2,1)S(1)} custom-call(s32[1024,128]{1,0:T(8,128)S(1)} %get-tuple-element.17.places_ref, bf16[128,4,8,128]{3,2,1,0:T(8,128)(2,1)S(1)} %all_to_all.10.x_ref), custom_call_target="tpu_custom_call" | custom-call | flops 1100000000 | bytes 2000000 | tf_op jit(solution)/shard_map/choose/pallas_call | solution.py:223
  77.3 19.1 %all_to_all.11.x_ref = bf16[4,4,256,128]{3,2,1,0:T(8,128)(2,1)S(1)} all-to-all(bf16[4,4,256,128]{3,2,1,0:T(8,128)(2,1)S(1)} %choose.1), channel_id=1, replica_groups={{1,2,3,0},{5,6,7,4},{9,10,11,8},{13,14,15,12},{17,18,19,16},{21,22,23,2..., dimensions={0} | all-to-all | bytes 2097152 | tf_op jit(solution)/shard_map/all_to_all | solution.py:33
  96.4 1.6 %correlate.1 = f32[1,2,2,256,256]{4,3,2,1,0:T(8,128)} custom-call(s32[4,256]{1,0:T(4,128)S(1)} %get-tuple-element.13.allocation_ref, bf16[4,4,256,128]{3,2,1,0:T(8,128)(2,1)S(1)} %all_to_all.11.x_ref), custom_call_target="tpu_custom_call" | custom-call | flops 540000000 | bytes 2000000 | tf_op jit(solution)/shard_map/correlate/pallas_call | solution.py:263
Async XLA Ops:
  1.5 5.5 %collective-permute-start = (bf16[2,8,2816]{2,1,0:T(8,128)(2,1)S(1)}, bf16[2,8,2816]{2,1,0:T(8,128)(2,1)S(1)}, u32[]{:S(2)}, u32[]{:S(2)}) collective-permute-start(bf16[2,8,2816]{2,1,0:T(8,128)(2,1)S(1)} %get-tuple-element.19), channel_id=1, source_target_pairs={{0,1},{1,2},{2,3},{4,5},{5,6},{6,7},{8,9},{9,10},{10,11},{12,13},{... | collective-permute-start | bytes 270344 | tf_op jit(solution)/shard_map/ppermute | solution.py:25

commit v4 on v3

--- a/solution.py
+++ b/solution.py
@@ -10,8 +10,8 @@
 
 LANES = 128
 BLOCK = 16
-WIDE_FIRST = 76
-TM_FIRST = 1
+WIDE_FIRST = 84
+TM_FIRST = 2
 IN_VMEM = pl.BlockSpec(memory_space=pltpu.VMEM)
 IN_HBM = pl.BlockSpec(memory_space=pltpu.HBM)
 IN_SMEM = pl.BlockSpec(memory_space=pltpu.SMEM)
@@ -25,8 +25,21 @@
     return lax.ppermute(value, axis, [(source, source + steps) for source in range(initial, last)])
 
 
-def member_order(count, first):
+def rolled(count, first):
     return [(first + step) % count for step in range(count)]
+
+
+def interleaved(count, first):
+    return [(first + step // 2 + step % 2 * (count // 2)) % count for step in range(count)]
+
+
+def interleaved_place(signal, signals, count, first):
+    half = signals * count // 2
+    ahead = signal - first * signals
+    ahead = jnp.where(ahead < 0, ahead + 2 * half, ahead)
+    far = ahead >= half
+    near = jnp.where(far, ahead - half, ahead)
+    return 2 * near - near % signals + jnp.where(far, signals, 0)
 
 
 def exchange(value, axis, order):
@@ -44,28 +57,50 @@
     return table.reshape(2 * length, 2 * length).astype(jnp.bfloat16)
 
 
-def stage_kernel(x_ref, *refs):
-    count = len(refs) // 2
-    sources, tail_out, targets, sems = refs[: count - 1], refs[count - 1], refs[count:-1], refs[-1]
+def place_rows(stations_ref, places_ref, order, place):
+    members = stations_ref.shape[1]
+    for block, sub in enumerate(order):
+        line = stations_ref[sub : sub + 1, :].astype(jnp.float32)
+        station = jnp.broadcast_to(line, (members, members)).T.astype(jnp.int32)
+        for pol in range(2):
+            places_ref[pl.ds(block * 2 * members + pol, members, stride=2), :] = place(2 * station + pol)
+
+
+def stage_kernel(x_ref, taps_ref, stations_ref, allocation_ref, tail_out, x_out, taps_out, allocation_out, places_out,
+                 stations, sems, *, order, place):
     first = x_ref.shape[2] - tail_out.shape[2]
-    copies = [pltpu.make_async_copy(x_ref.at[:, :, first:], tail_out, sems.at[0])]
-    for place, (source, target) in enumerate(zip((x_ref,) + sources, targets)):
-        copies.append(pltpu.make_async_copy(source, target, sems.at[place + 1]))
+    pairs = [
+        (stations_ref, stations),
+        (x_ref.at[:, :, first:], tail_out),
+        (x_ref, x_out),
+        (taps_ref, taps_out),
+        (allocation_ref, allocation_out),
+    ]
+    copies = [pltpu.make_async_copy(*pair, sems.at[which]) for which, pair in enumerate(pairs)]
     for copy in copies:
         copy.start()
-    for copy in copies:
+    copies[0].wait()
+    place_rows(stations, places_out, order, place)
+    for copy in copies[1:]:
         copy.wait()
 
 
-def stage(tail_length, *operands):
-    tail = operands[0].shape[:2] + (tail_length,)
-    return pl.pallas_call(
-        stage_kernel,
-        in_specs=[IN_HBM] * len(operands),
-        out_specs=[IN_VMEM] * (len(operands) + 1),
-        out_shape=[pltpu.VMEM(tail, operands[0].dtype)]
-        + [pltpu.VMEM(value.shape, value.dtype) for value in operands],
-        scratch_shapes=[pltpu.SemaphoreType.DMA((len(operands) + 1,))],
+def stage(voltages, filter_taps, stations, allocation, **rows):
+    taps, length = filter_taps.shape
+    members = stations.shape[1]
+    operands = [voltages, filter_taps, stations, allocation]
+    return pl.pallas_call(
+        lambda *refs: stage_kernel(*refs, **rows),
+        in_specs=[IN_HBM] * 4,
+        out_specs=[IN_VMEM] * 5,
+        out_shape=[
+            pltpu.VMEM(voltages.shape[:2] + ((taps - 1) * length,), voltages.dtype),
+            pltpu.VMEM(voltages.shape, voltages.dtype),
+            pltpu.VMEM(filter_taps.shape, filter_taps.dtype),
+            pltpu.VMEM(allocation.shape, allocation.dtype),
+            pltpu.VMEM((2 * stations.size, members), jnp.int32),
+        ],
+        scratch_shapes=[pltpu.VMEM(stations.shape, stations.dtype), pltpu.SemaphoreType.DMA((5,))],
         compiler_params=PARAMS,
         name="stage",
     )(*[pltpu.with_memory_space_constraint(value, pltpu.HBM) for value in operands])
@@ -90,19 +125,9 @@
     return total
 
 
-def place_rows(stations_ref, places_ref, order, first, total):
-    members = stations_ref.shape[1]
-    for block, sub in enumerate(order):
-        line = stations_ref[sub : sub + 1, :].astype(jnp.float32)
-        station = jnp.broadcast_to(line, (members, members)).T.astype(jnp.int32)
-        for pol in range(2):
-            place = 2 * station + (pol - first)
-            place = jnp.where(place < 0, place + total, place)
-            places_ref[pl.ds(block * 2 * members + pol, members, stride=2), :] = place
-
-
-def filter_kernel(x_ref, taps_ref, stations_ref, out_ref, places_ref, *, order, first, total):
-    place_rows(stations_ref, places_ref, order, first, total)
+def filter_kernel(x_ref, taps_ref, table_ref, out_ref, table_out, sem):
+    copy = pltpu.make_async_copy(table_ref, table_out, sem)
+    copy.start()
     taps, length = taps_ref.shape
     signals = x_ref.shape[1]
     cols = length // LANES
@@ -125,22 +150,23 @@
                 load_frame(x_ref, part, BLOCK - (taps - 1) + frame, col, cols) for frame in range(taps - 1)
             )
             lax.fori_loop(1, frames // BLOCK, step, opening, unroll=frames // BLOCK - 1)
-
-
-def filter_body(x, filter_taps, stations, **places):
+    copy.wait()
+
+
+def filter_body(x, filter_taps, table):
     _, signals, samples = x.shape
     length = filter_taps.shape[1]
-    members = stations.shape[1]
     shape = (2, length // LANES, signals * (samples // length), LANES)
     return pl.pallas_call(
-        lambda *refs: filter_kernel(*refs, **places),
-        in_specs=[IN_VMEM] * 3,
+        filter_kernel,
+        in_specs=[IN_VMEM, IN_VMEM, IN_HBM],
         out_specs=[IN_VMEM] * 2,
-        out_shape=[pltpu.VMEM(shape, jnp.float32), pltpu.VMEM((2 * stations.size, members), jnp.int32)],
+        out_shape=[pltpu.VMEM(shape, jnp.float32), pltpu.VMEM(table.shape, table.dtype)],
+        scratch_shapes=[pltpu.SemaphoreType.DMA(())],
         compiler_params=PARAMS,
         cost_estimate=pl.CostEstimate(flops=12_000_000, bytes_accessed=6_000_000, transcendentals=0),
         name="filter_body",
-    )(x, filter_taps, stations)
+    )(x, filter_taps, pltpu.with_memory_space_constraint(table, pltpu.HBM))
 
 
 def transform_kernel(body_ref, halo_ref, x_ref, taps_ref, table_ref, out_ref, opening, turned):
@@ -273,21 +299,24 @@
 
 
 def shards(voltages, filter_taps, stations, allocation):
-    num_taps, length = filter_taps.shape
+    length = filter_taps.shape[1]
     signals = voltages.shape[1]
     frames = voltages.shape[2] // length
     owners = lax.axis_size("wide")
-    wide_order = member_order(owners, WIDE_FIRST % owners)
-    tm_order = member_order(lax.axis_size("tm"), TM_FIRST % lax.axis_size("tm"))
-
-    table = jnp.asarray(transform_table(length, wide_order))
-    tail, x, taps, table, stations, allocation = stage(
-        (num_taps - 1) * length, voltages, filter_taps, table, stations, allocation
+    first = WIDE_FIRST % owners
+    wide_order = interleaved(owners, first)
+    tm_order = rolled(lax.axis_size("tm"), TM_FIRST % lax.axis_size("tm"))
+
+    tail, x, taps, allocation, places = stage(
+        voltages,
+        filter_taps,
+        stations,
+        allocation,
+        order=tm_order,
+        place=lambda signal: interleaved_place(signal, signals, owners, first),
     )
     halo = shifted(tail, "tm", 1)
-    body, places = filter_body(
-        x, taps, stations, order=tm_order, first=wide_order[0] * signals, total=owners * signals
-    )
+    body, table = filter_body(x, taps, jnp.asarray(transform_table(length, wide_order)))
     spectra = transform(body, halo, x, taps, table)
     spectra = spectra.reshape(owners, 2 * length // owners, signals, frames)
     turned = exchange(spectra, "wide", wide_order)

time: 99.2 us -> 97.9 us (0.987)
  no operation moved by 1% of the time
where the time goes in v4:
time: 97.9 us; the launch traced here: 97.2 us
  blocking collectives  86.4 us (88%)
  Pallas kernels  6.85 us (7%)
  starting transfers between devices  3.4 us (3%)
    all_to_all x2, blocking collectives, exchange(): lax.all_to_all(value, axis, split_axis=0, concat_axis=0, tiled=True, axis...  86.4 us
    ppermute x1, starting transfers between devices, shifted(): lax.ppermute(value, axis, [(source, source + steps) for source in range(i...  3.4 us
  transfers between devices with their start and end apart: 1, of which 1 were waited for; matrix products, arithmetic and copies ran while one was open for 0% of the time, Pallas kernels for 2%

profile of v4, /device:TPU:24, one launch (start us, length us, event | category | flops | bytes accessed | tf_op | source)
XLA Modules:
  0.0 97.2 jit_solution(7827287741995146651)
XLA Ops:
  0.0 1.4 %stage.1 = (bf16[2,8,2816]{2,1,0:T(8,128)(2,1)S(1)}, bf16[2,8,32768]{2,1,0:T(8,128)(2,1)S(1)}, f32[12,256]{1,0:T(8,128)S(1)}, s32[4,256]{1,0:T(4,128)S(1)}, s32[1024,128]{1,0:T(8,128)S(1)}) custom-call(bf16[2,8,32768]{2,1,0:T(8,128)(2,1)} %refs_0_.1, f32[12,256]{1,0:T(8,128)} %refs_1_.1, s32[4,128]{1,0:T(4,128)} %refs_2_.1, s32[4,256]{1,0:T(4,128)} %refs_3_.1), custom_call_target="tpu_custom_call" | custom-call | tf_op jit(solution)/shard_map/stage/pallas_call | solution.py:92
  1.4 3.4 %collective-permute-start = (bf16[2,8,2816]{2,1,0:T(8,128)(2,1)S(1)}, bf16[2,8,2816]{2,1,0:T(8,128)(2,1)S(1)}, u32[]{:S(2)}, u32[]{:S(2)}) collective-permute-start(bf16[2,8,2816]{2,1,0:T(8,128)(2,1)S(1)} %get-tuple-element.17), channel_id=1, source_target_pairs={{0,1},{1,2},{2,3},{4,5},{5,6},{6,7},{8,9},{9,10},{10,11},{12,13},{... | collective-permute-start | bytes 270344 | tf_op jit(solution)/shard_map/ppermute | solution.py:25
  4.8 1.6 %filter_body.1 = (f32[2,2,1024,128]{3,2,1,0:T(8,128)S(1)}, bf16[512,512]{1,0:T(8,128)(2,1)S(1)}) custom-call(bf16[2,8,32768]{2,1,0:T(8,128)(2,1)S(1)} %get-tuple-element.14.x_ref, f32[12,256]{1,0:T(8,128)S(1)} %get-tuple-element.15.taps_ref, bf16[512,512]{1,0:T(8,128)(2,1)} %constant.2.clone.table_ref), custom_call_target="tpu_custom_call" | custom-call | flops 12000000 | bytes 6000000 | tf_op jit(solution)/shard_map/filter_body/pallas_call | solution.py:160
  6.4 0.5 collective-permute-done.halo_ref
  6.9 1.0 %transform.1 = bf16[512,8,128]{2,1,0:T(8,128)(2,1)S(1)} custom-call(f32[2,2,1024,128]{3,2,1,0:T(8,128)S(1)} %get-tuple-element.16.body_ref, bf16[2,8,2816]{2,1,0:T(8,128)(2,1)S(1)} %collective-permute-done.halo_ref, bf16[2,8,32768]{2,1,0:T(8,128)(2,1)S(1)} %get-tuple-element.14.x_ref, f32[12,256]{1,0:T(8,128)S(1)} %get-tuple-element.15.taps_ref, ...), custom_call_target="tpu_custom_call" | custom-call | flops 540000000 | bytes 4000000 | tf_op jit(solution)/shard_map/transform/pallas_call | solution.py:210
  7.9 66.9 %all_to_all.10.x_ref = bf16[128,4,8,128]{3,2,1,0:T(8,128)(2,1)S(1)} all-to-all(bf16[128,4,8,128]{3,2,1,0:T(8,128)(2,1)S(1)} %bitcast.1), channel_id=1, replica_groups={{336,80,340,84,344,88,348,92,352,96,356,100,360,104,364,108,368,112,372..., dimensions={0} | all-to-all | bytes 2097152 | tf_op jit(solution)/shard_map/all_to_all | solution.py:46
  74.9 1.2 %choose.1 = bf16[4,4,256,128]{3,2,1,0:T(8,128)(2,1)S(1)} custom-call(s32[1024,128]{1,0:T(8,128)S(1)} %get-tuple-element.13.places_ref, bf16[128,4,8,128]{3,2,1,0:T(8,128)(2,1)S(1)} %all_to_all.10.x_ref), custom_call_target="tpu_custom_call" | custom-call | flops 1100000000 | bytes 2000000 | tf_op jit(solution)/shard_map/choose/pallas_call | solution.py:249
  76.1 19.5 %all_to_all.11.x_ref = bf16[4,4,256,128]{3,2,1,0:T(8,128)(2,1)S(1)} all-to-all(bf16[4,4,256,128]{3,2,1,0:T(8,128)(2,1)S(1)} %choose.1), channel_id=1, replica_groups={{2,3,0,1},{6,7,4,5},{10,11,8,9},{14,15,12,13},{18,19,16,17},{22,23,20,2..., dimensions={0} | all-to-all | bytes 2097152 | tf_op jit(solution)/shard_map/all_to_all | solution.py:46
  95.6 1.6 %correlate.1 = f32[1,2,2,256,256]{4,3,2,1,0:T(8,128)} custom-call(s32[4,256]{1,0:T(4,128)S(1)} %get-tuple-element.12.allocation_ref, bf16[4,4,256,128]{3,2,1,0:T(8,128)(2,1)S(1)} %all_to_all.11.x_ref), custom_call_target="tpu_custom_call" | custom-call | flops 540000000 | bytes 2000000 | tf_op jit(solution)/shard_map/correlate/pallas_call | solution.py:289
Async XLA Ops:
  1.4 5.5 %collective-permute-start = (bf16[2,8,2816]{2,1,0:T(8,128)(2,1)S(1)}, bf16[2,8,2816]{2,1,0:T(8,128)(2,1)S(1)}, u32[]{:S(2)}, u32[]{:S(2)}) collective-permute-start(bf16[2,8,2816]{2,1,0:T(8,128)(2,1)S(1)} %get-tuple-element.17), channel_id=1, source_target_pairs={{0,1},{1,2},{2,3},{4,5},{5,6},{6,7},{8,9},{9,10},{10,11},{12,13},{... | collective-permute-start | bytes 270344 | tf_op jit(solution)/shard_map/ppermute | solution.py:25

commit v5 on v4

--- a/solution.py
+++ b/solution.py
@@ -11,7 +11,7 @@
 LANES = 128
 BLOCK = 16
 WIDE_FIRST = 84
-TM_FIRST = 2
+ORDER = ((2,), (1, 3), (0,))
 IN_VMEM = pl.BlockSpec(memory_space=pltpu.VMEM)
 IN_HBM = pl.BlockSpec(memory_space=pltpu.HBM)
 IN_SMEM = pl.BlockSpec(memory_space=pltpu.SMEM)
@@ -23,10 +23,6 @@
     count = lax.axis_size(axis)
     initial, last = (max(0, -steps), min(count, count - steps))
     return lax.ppermute(value, axis, [(source, source + steps) for source in range(initial, last)])
-
-
-def rolled(count, first):
-    return [(first + step) % count for step in range(count)]
 
 
 def interleaved(count, first):
@@ -40,6 +36,11 @@
     far = ahead >= half
     near = jnp.where(far, ahead - half, ahead)
     return 2 * near - near % signals + jnp.where(far, signals, 0)
+
+
+def paired(value, axis, steps):
+    count = lax.axis_size(axis)
+    return lax.ppermute(value, axis, [(source, source ^ steps) for source in range(count)])
 
 
 def exchange(value, axis, order):
@@ -57,17 +58,18 @@
     return table.reshape(2 * length, 2 * length).astype(jnp.bfloat16)
 
 
-def place_rows(stations_ref, places_ref, order, place):
-    members = stations_ref.shape[1]
-    for block, sub in enumerate(order):
-        line = stations_ref[sub : sub + 1, :].astype(jnp.float32)
+def place_rows(stations_ref, places_ref, place):
+    subs, members = stations_ref.shape
+    own = lax.axis_index("tm")
+    for block in range(subs):
+        line = stations_ref[pl.ds(own ^ block, 1), :].astype(jnp.float32)
         station = jnp.broadcast_to(line, (members, members)).T.astype(jnp.int32)
         for pol in range(2):
             places_ref[pl.ds(block * 2 * members + pol, members, stride=2), :] = place(2 * station + pol)
 
 
 def stage_kernel(x_ref, taps_ref, stations_ref, allocation_ref, tail_out, x_out, taps_out, allocation_out, places_out,
-                 stations, sems, *, order, place):
+                 stations, sems, *, place):
     first = x_ref.shape[2] - tail_out.shape[2]
     pairs = [
         (stations_ref, stations),
@@ -80,7 +82,7 @@
     for copy in copies:
         copy.start()
     copies[0].wait()
-    place_rows(stations, places_out, order, place)
+    place_rows(stations, places_out, place)
     for copy in copies[1:]:
         copy.wait()
 
@@ -222,16 +224,17 @@
     )(body, halo, x, filter_taps, table)
 
 
-def choose_kernel(places_ref, x_ref, out_ref):
+def choose_kernel(places_ref, x_ref, *out_refs, blocks):
     sources, parts, signals, frames = x_ref.shape
-    subs, _, members, _ = out_ref.shape
+    out_refs = out_refs[-len(blocks) :]
+    members = out_refs[0].shape[1]
     width = places_ref.shape[1]
     columns = jnp.concatenate(
         [x_ref[:, part].reshape(sources * signals, frames) for part in range(parts)], axis=1
     )
     lane = lax.broadcasted_iota(jnp.int32, (members, width), 1)
-    for sub in range(subs):
-        wanted = places_ref[sub * members : (sub + 1) * members, :]
+    for block, out_ref in zip(blocks, out_refs):
+        wanted = places_ref[block * members : (block + 1) * members, :]
         pick = jnp.concatenate(
             [
                 jnp.where(wanted == lane + start, 1.0, 0.0).astype(jnp.bfloat16)
@@ -241,38 +244,68 @@
         )
         chosen = jnp.dot(pick, columns, preferred_element_type=jnp.float32).astype(jnp.bfloat16)
         for part in range(parts):
-            out_ref[sub, part] = chosen[:, part * frames : (part + 1) * frames]
-
-
-def choose(places, turned, subs):
+            out_ref[part] = chosen[:, part * frames : (part + 1) * frames]
+
+
+def choose(places, turned, members, blocks, after=()):
     _, parts, _, frames = turned.shape
     return pl.pallas_call(
-        choose_kernel,
-        in_specs=[IN_VMEM] * 2,
+        lambda *refs: choose_kernel(*refs, blocks=blocks),
+        in_specs=[IN_VMEM] * (2 + len(after)),
+        out_specs=[IN_VMEM] * len(blocks),
+        out_shape=[pltpu.VMEM((parts, members, frames), jnp.bfloat16)] * len(blocks),
+        compiler_params=PARAMS,
+        cost_estimate=pl.CostEstimate(
+            flops=270_000_000 * len(blocks), bytes_accessed=1_000_000 * len(blocks), transcendentals=0
+        ),
+        name="choose",
+    )(places, turned, *after)
+
+
+def stacked(x_refs, channel):
+    real = [segment[2 * channel] for segment in x_refs]
+    imag = [segment[2 * channel + 1] for segment in x_refs]
+    left = jnp.concatenate(real + imag, axis=1)
+    return left, (left, jnp.concatenate(imag + [-value for value in real], axis=1))
+
+
+def begin_kernel(*refs):
+    x_refs, out_ref = refs[:-1], refs[-1]
+    for channel in range(out_ref.shape[0]):
+        left, both = stacked(x_refs, channel)
+        for part, rows in enumerate(both):
+            out_ref[channel, part] = lax.dot_general(rows, left, CONTRACT_LAST, preferred_element_type=jnp.float32)
+
+
+def begin(gathered):
+    parts, members, _ = gathered[0].shape
+    return pl.pallas_call(
+        begin_kernel,
+        in_specs=[IN_VMEM] * len(gathered),
         out_specs=IN_VMEM,
-        out_shape=pltpu.VMEM((subs, parts, places.shape[0] // subs, frames), jnp.bfloat16),
-        compiler_params=PARAMS,
-        cost_estimate=pl.CostEstimate(flops=1_100_000_000, bytes_accessed=2_000_000, transcendentals=0),
-        name="choose",
-    )(places, turned)
-
-
-def correlate_kernel(allocation_ref, x_ref, out_ref, grams, sems):
-    segments, parts, _, frames = x_ref.shape
+        out_shape=pltpu.VMEM((parts // 2, 2, members, members), jnp.float32),
+        compiler_params=PARAMS,
+        cost_estimate=pl.CostEstimate(flops=270_000_000, bytes_accessed=2_000_000, transcendentals=0),
+        name="begin",
+    )(*gathered)
+
+
+def correlate_kernel(allocation_ref, begun_ref, *refs):
+    x_refs, (out_ref, grams, sems) = refs[:-3], refs[-3:]
+    parts, _, frames = x_refs[0].shape
     channels = parts // 2
     first = lax.axis_index("wide") * channels
-    row = allocation_ref[pl.ds(lax.axis_index("tm"), 1), :].astype(jnp.float32) * (1.0 / (frames * segments))
+    scale = 1.0 / (frames * lax.axis_size("tm"))
+    row = allocation_ref[pl.ds(lax.axis_index("tm"), 1), :].astype(jnp.float32) * scale
     lane = lax.broadcasted_iota(jnp.int32, row.shape, 1)
     copies = []
     for channel in range(channels):
-        real = [x_ref[segment, 2 * channel] for segment in range(segments)]
-        imag = [x_ref[segment, 2 * channel + 1] for segment in range(segments)]
-        left = jnp.concatenate(real + imag, axis=1)
-        turned = jnp.concatenate(imag + [-value for value in real], axis=1)
+        left, both = stacked(x_refs, channel)
         weight = jnp.sum(jnp.where(lane == first + channel, row, 0.0), axis=1, keepdims=True)
-        for part, rows in enumerate((left, turned)):
-            grams[channel, part] = weight * lax.dot_general(
-                rows, left, CONTRACT_LAST, preferred_element_type=jnp.float32
+        for part, rows in enumerate(both):
+            grams[channel, part] = weight * (
+                begun_ref[channel, part]
+                + lax.dot_general(rows, left, CONTRACT_LAST, preferred_element_type=jnp.float32)
             )
             copy = pltpu.make_async_copy(
                 grams.at[channel, part], out_ref.at[0, channel, part], sems.at[2 * channel + part]
@@ -283,19 +316,19 @@
         copy.wait()
 
 
-def correlate(allocation, gathered):
-    _, parts, members, _ = gathered.shape
+def correlate(allocation, begun, gathered):
+    parts, members, _ = gathered[0].shape
     shape = (parts // 2, 2, members, members)
     return pl.pallas_call(
         correlate_kernel,
-        in_specs=[IN_VMEM, IN_VMEM],
+        in_specs=[IN_VMEM] * (2 + len(gathered)),
         out_specs=IN_HBM,
         out_shape=jax.ShapeDtypeStruct((1,) + shape, jnp.float32),
         scratch_shapes=[pltpu.VMEM(shape, jnp.float32), pltpu.SemaphoreType.DMA((parts,))],
         compiler_params=PARAMS,
-        cost_estimate=pl.CostEstimate(flops=540_000_000, bytes_accessed=2_000_000, transcendentals=0),
+        cost_estimate=pl.CostEstimate(flops=270_000_000, bytes_accessed=2_000_000, transcendentals=0),
         name="correlate",
-    )(allocation, gathered)
+    )(allocation, begun, *gathered)
 
 
 def shards(voltages, filter_taps, stations, allocation):
@@ -305,14 +338,12 @@
     owners = lax.axis_size("wide")
     first = WIDE_FIRST % owners
     wide_order = interleaved(owners, first)
-    tm_order = rolled(lax.axis_size("tm"), TM_FIRST % lax.axis_size("tm"))
 
     tail, x, taps, allocation, places = stage(
         voltages,
         filter_taps,
         stations,
         allocation,
-        order=tm_order,
         place=lambda signal: interleaved_place(signal, signals, owners, first),
     )
     halo = shifted(tail, "tm", 1)
@@ -320,8 +351,12 @@
     spectra = transform(body, halo, x, taps, table)
     spectra = spectra.reshape(owners, 2 * length // owners, signals, frames)
     turned = exchange(spectra, "wide", wide_order)
-    chosen = choose(places, turned, stations.shape[0])
-    return correlate(allocation, exchange(chosen, "tm", tm_order))
+    members = 2 * stations.shape[1]
+    met, after = [], ()
+    for blocks in ORDER:
+        after = choose(places, turned, members, blocks, after[:1])
+        met += [paired(value, "tm", block) if block else value for block, value in zip(blocks, after)]
+    return correlate(allocation, begin([met[-1], met[0]]), met[1:-1])
 
 
 def solution(mesh):

time: 97.9 us -> 96.6 us (0.987)
  blocking collectives: 86.4 us -> 66.9 us
  starting transfers between devices: 3.4 us -> 14.2 us
  waiting for transfers between devices: 0.47 us -> 7.74 us
    all_to_all x2 -> x1, blocking collectives: 86.4 us -> 66.9 us  [exchange(): lax.all_to_all(value, axis, split_axis=0, concat_axis=0, tiled=True, axis...]
    ppermute x0 -> x3, starting transfers between devices: none -> 10.8 us  [paired(): lax.ppermute(value, axis, [(source, source ^ steps) for source in range(c...]
    ppermute x0 -> x3, waiting for transfers between devices: none -> 7.27 us  [paired(): lax.ppermute(value, axis, [(source, source ^ steps) for source in range(c...]
    pallas_call x2 -> x5, Pallas kernels: 2.81 us -> 3.38 us  [the longest x3 1.57 us: choose(): pl.pallas_call(lambda *refs: choose_kernel(*refs, blocks=blocks), in_spec...]
  transfers between devices with their start and end apart: 1 -> 4, of which waited for: 1 -> 4; matrix products, arithmetic and copies ran while one was open for 0% -> 0% of each run, Pallas kernels for 2% -> 3%
where the time goes in v5:
time: 96.6 us; the launch traced here: 96.4 us
  blocking collectives  66.9 us (69%)
  starting transfers between devices  14.2 us (15%)
  waiting for transfers between devices  7.74 us (8%)
  Pallas kernels  7.42 us (8%)
    all_to_all x1, blocking collectives, exchange(): lax.all_to_all(value, axis, split_axis=0, concat_axis=0, tiled=True, axis...  66.9 us
    ppermute x3, starting transfers between devices, paired(): lax.ppermute(value, axis, [(source, source ^ steps) for source in range(c...  10.8 us
    ppermute x3, waiting for transfers between devices, paired(): lax.ppermute(value, axis, [(source, source ^ steps) for source in range(c...  7.27 us
    ppermute x1, starting transfers between devices, shifted(): lax.ppermute(value, axis, [(source, source + steps) for source in range(i...  3.4 us
  transfers between devices with their start and end apart: 4, of which 4 were waited for; matrix products, arithmetic and copies ran while one was open for 0% of the time, Pallas kernels for 3%

profile of v5, /device:TPU:24, one launch (start us, length us, event | category | flops | bytes accessed | tf_op | source)
XLA Modules:
  0.0 96.4 jit_solution(1698567065176859168)
XLA Ops:
  0.0 1.4 %stage.1 = (bf16[2,8,2816]{2,1,0:T(8,128)(2,1)S(1)}, bf16[2,8,32768]{2,1,0:T(8,128)(2,1)S(1)}, f32[12,256]{1,0:T(8,128)S(1)}, s32[4,256]{1,0:T(4,128)S(1)}, s32[1024,128]{1,0:T(8,128)S(1)}) custom-call(bf16[2,8,32768]{2,1,0:T(8,128)(2,1)} %refs_0_.1, f32[12,256]{1,0:T(8,128)} %refs_1_.1, s32[4,128]{1,0:T(4,128)} %refs_2_.1, s32[4,256]{1,0:T(4,128)} %refs_3_.1), custom_call_target="tpu_custom_call" | custom-call | tf_op jit(solution)/shard_map/stage/pallas_call | solution.py:94
  1.4 3.4 %collective-permute-start = (bf16[2,8,2816]{2,1,0:T(8,128)(2,1)S(1)}, bf16[2,8,2816]{2,1,0:T(8,128)(2,1)S(1)}, u32[]{:S(2)}, u32[]{:S(2)}) collective-permute-start(bf16[2,8,2816]{2,1,0:T(8,128)(2,1)S(1)} %get-tuple-element.19), channel_id=1, source_target_pairs={{0,1},{1,2},{2,3},{4,5},{5,6},{6,7},{8,9},{9,10},{10,11},{12,13},{... | collective-permute-start | bytes 270344 | tf_op jit(solution)/shard_map/ppermute | solution.py:25
  4.8 1.6 %filter_body.1 = (f32[2,2,1024,128]{3,2,1,0:T(8,128)S(1)}, bf16[512,512]{1,0:T(8,128)(2,1)S(1)}) custom-call(bf16[2,8,32768]{2,1,0:T(8,128)(2,1)S(1)} %get-tuple-element.16.x_ref, f32[12,256]{1,0:T(8,128)S(1)} %get-tuple-element.17.taps_ref, bf16[512,512]{1,0:T(8,128)(2,1)} %constant.2.clone.table_ref), custom_call_target="tpu_custom_call" | custom-call | flops 12000000 | bytes 6000000 | tf_op jit(solution)/shard_map/filter_body/pallas_call | solution.py:162
  6.4 0.5 collective-permute-done.halo_ref
  6.9 1.0 %transform.1 = bf16[512,8,128]{2,1,0:T(8,128)(2,1)S(1)} custom-call(f32[2,2,1024,128]{3,2,1,0:T(8,128)S(1)} %get-tuple-element.18.body_ref, bf16[2,8,2816]{2,1,0:T(8,128)(2,1)S(1)} %collective-permute-done.halo_ref, bf16[2,8,32768]{2,1,0:T(8,128)(2,1)S(1)} %get-tuple-element.16.x_ref, f32[12,256]{1,0:T(8,128)S(1)} %get-tuple-element.17.taps_ref, ...), custom_call_target="tpu_custom_call" | custom-call | flops 540000000 | bytes 4000000 | tf_op jit(solution)/shard_map/transform/pallas_call | solution.py:212
  7.9 66.9 %all_to_all.5.refs_1_ = bf16[128,4,8,128]{3,2,1,0:T(8,128)(2,1)S(1)} all-to-all(bf16[128,4,8,128]{3,2,1,0:T(8,128)(2,1)S(1)} %bitcast.1), channel_id=1, replica_groups={{336,80,340,84,344,88,348,92,352,96,356,100,360,104,364,108,368,112,372..., dimensions={0} | all-to-all | bytes 2097152 | tf_op jit(solution)/shard_map/all_to_all | solution.py:47
  74.9 0.4 choose.3.refs_2_
  75.3 5.8 %collective-permute-start.1 = (bf16[4,256,128]{2,1,0:T(8,128)(2,1)S(1)}, bf16[4,256,128]{2,1,0:T(8,128)(2,1)S(1)}, u32[]{:S(2)}, u32[]{:S(2)}) collective-permute-start(bf16[4,256,128]{2,1,0:T(8,128)(2,1)S(1)} %choose.3.refs_2_), channel_id=1, source_target_pairs={{0,2},{1,3},{2,0},{3,1},{4,6},{5,7},{6,4},{7,5},{8,10},{9,11},{10,... | collective-permute-start | bytes 786440 | tf_op jit(solution)/shard_map/ppermute | solution.py:43
  81.2 0.7 choose.4
  81.9 3.0 %collective-permute-start.3 = (bf16[4,256,128]{2,1,0:T(8,128)(2,1)S(1)}, bf16[4,256,128]{2,1,0:T(8,128)(2,1)S(1)}, u32[]{:S(2)}, u32[]{:S(2)}) collective-permute-start(bf16[4,256,128]{2,1,0:T(8,128)(2,1)S(1)} %get-tuple-element.22), channel_id=1, source_target_pairs={{0,3},{1,2},{2,1},{3,0},{4,7},{5,6},{6,5},{7,4},{8,11},{9,10},{10,... | collective-permute-start | bytes 786440 | tf_op jit(solution)/shard_map/ppermute | solution.py:43
  84.9 1.9 %collective-permute-start.2 = (bf16[4,256,128]{2,1,0:T(8,128)(2,1)S(1)}, bf16[4,256,128]{2,1,0:T(8,128)(2,1)S(1)}, u32[]{:S(2)}, u32[]{:S(2)}) collective-permute-start(bf16[4,256,128]{2,1,0:T(8,128)(2,1)S(1)} %get-tuple-element.21.refs_2_), channel_id=1, source_target_pairs={{0,1},{1,0},{2,3},{3,2},{4,5},{5,4},{6,7},{7,6},{8,9},{9,8},{10,11... | collective-permute-start | bytes 786440 | tf_op jit(solution)/shard_map/ppermute | solution.py:43
  86.9 0.4 choose.5.refs_0_
  87.3 0.9 collective-permute-done.1.refs_1_
  88.2 0.5 begin.1.begun_ref
  88.7 5.1 %collective-permute-done.3.refs_1_ = bf16[4,256,128]{2,1,0:T(8,128)(2,1)S(1)} collective-permute-done((bf16[4,256,128]{2,1,0:T(8,128)(2,1)S(1)}, bf16[4,256,128]{2,1,0:T(8,128)(2,1)S(1)}, u32[]{:S(2)}, u32[]{:S(2)}) %collective-permute-start.3) | collective-permute-done | bytes 262176 | tf_op jit(solution)/shard_map/ppermute | solution.py:43
  93.8 1.2 %collective-permute-done.2.refs_0_ = bf16[4,256,128]{2,1,0:T(8,128)(2,1)S(1)} collective-permute-done((bf16[4,256,128]{2,1,0:T(8,128)(2,1)S(1)}, bf16[4,256,128]{2,1,0:T(8,128)(2,1)S(1)}, u32[]{:S(2)}, u32[]{:S(2)}) %collective-permute-start.2) | collective-permute-done | bytes 262176 | tf_op jit(solution)/shard_map/ppermute | solution.py:43
  95.0 1.3 %correlate.1 = f32[1,2,2,256,256]{4,3,2,1,0:T(8,128)} custom-call(s32[4,256]{1,0:T(4,128)S(1)} %get-tuple-element.14.allocation_ref, f32[2,2,256,256]{3,2,1,0:T(8,128)S(1)} %begin.1.begun_ref, bf16[4,256,128]{2,1,0:T(8,128)(2,1)S(1)} %collective-permute-done.2.refs_0_, bf16[4,256,128]{2,1,0:T(8,128)(2,1)S(1)} %collective-permute-done.3.refs_1_), custom_call_target="tpu_custom_call" | custom-call | flops 270000000 | bytes 2000000 | tf_op jit(solution)/shard_map/correlate/pallas_call | solution.py:322
Async XLA Ops:
  1.4 5.5 %collective-permute-start = (bf16[2,8,2816]{2,1,0:T(8,128)(2,1)S(1)}, bf16[2,8,2816]{2,1,0:T(8,128)(2,1)S(1)}, u32[]{:S(2)}, u32[]{:S(2)}) collective-permute-start(bf16[2,8,2816]{2,1,0:T(8,128)(2,1)S(1)} %get-tuple-element.19), channel_id=1, source_target_pairs={{0,1},{1,2},{2,3},{4,5},{5,6},{6,7},{8,9},{9,10},{10,11},{12,13},{... | collective-permute-start | bytes 270344 | tf_op jit(solution)/shard_map/ppermute | solution.py:25
  75.3 12.9 %collective-permute-start.1 = (bf16[4,256,128]{2,1,0:T(8,128)(2,1)S(1)}, bf16[4,256,128]{2,1,0:T(8,128)(2,1)S(1)}, u32[]{:S(2)}, u32[]{:S(2)}) collective-permute-start(bf16[4,256,128]{2,1,0:T(8,128)(2,1)S(1)} %choose.3.refs_2_), channel_id=1, source_target_pairs={{0,2},{1,3},{2,0},{3,1},{4,6},{5,7},{6,4},{7,5},{8,10},{9,11},{10,... | collective-permute-start | bytes 786440 | tf_op jit(solution)/shard_map/ppermute | solution.py:43
  81.9 11.9 %collective-permute-start.3 = (bf16[4,256,128]{2,1,0:T(8,128)(2,1)S(1)}, bf16[4,256,128]{2,1,0:T(8,128)(2,1)S(1)}, u32[]{:S(2)}, u32[]{:S(2)}) collective-permute-start(bf16[4,256,128]{2,1,0:T(8,128)(2,1)S(1)} %get-tuple-element.22), channel_id=1, source_target_pairs={{0,3},{1,2},{2,1},{3,0},{4,7},{5,6},{6,5},{7,4},{8,11},{9,10},{10,... | collective-permute-start | bytes 786440 | tf_op jit(solution)/shard_map/ppermute | solution.py:43
  84.9 10.1 %collective-permute-start.2 = (bf16[4,256,128]{2,1,0:T(8,128)(2,1)S(1)}, bf16[4,256,128]{2,1,0:T(8,128)(2,1)S(1)}, u32[]{:S(2)}, u32[]{:S(2)}) collective-permute-start(bf16[4,256,128]{2,1,0:T(8,128)(2,1)S(1)} %get-tuple-element.21.refs_2_), channel_id=1, source_target_pairs={{0,1},{1,0},{2,3},{3,2},{4,5},{5,4},{6,7},{7,6},{8,9},{9,8},{10,11... | collective-permute-start | bytes 786440 | tf_op jit(solution)/shard_map/ppermute | solution.py:43

commit v6 on v5

--- a/solution.py
+++ b/solution.py
@@ -10,7 +10,7 @@
 
 LANES = 128
 BLOCK = 16
-WIDE_FIRST = 84
+WIDE_FIRST = 85
 ORDER = ((2,), (1, 3), (0,))
 IN_VMEM = pl.BlockSpec(memory_space=pltpu.VMEM)
 IN_HBM = pl.BlockSpec(memory_space=pltpu.HBM)

time: 96.6 us -> 96.4 us (level)
  no operation moved by 1% of the time
where the time goes in v6:
time: 96.4 us; the launch traced here: 96.2 us
  blocking collectives  66.6 us (69%)
  starting transfers between devices  14.2 us (15%)
  waiting for transfers between devices  7.79 us (8%)
  Pallas kernels  7.42 us (8%)
    all_to_all x1, blocking collectives, exchange(): lax.all_to_all(value, axis, split_axis=0, concat_axis=0, tiled=True, axis...  66.6 us
    ppermute x3, starting transfers between devices, paired(): lax.ppermute(value, axis, [(source, source ^ steps) for source in range(c...  10.8 us
    ppermute x3, waiting for transfers between devices, paired(): lax.ppermute(value, axis, [(source, source ^ steps) for source in range(c...  7.32 us
    ppermute x1, starting transfers between devices, shifted(): lax.ppermute(value, axis, [(source, source + steps) for source in range(i...  3.4 us
  transfers between devices with their start and end apart: 4, of which 4 were waited for; matrix products, arithmetic and copies ran while one was open for 0% of the time, Pallas kernels for 3%

profile of v6, /device:TPU:24, one launch (start us, length us, event | category | flops | bytes accessed | tf_op | source)
XLA Modules:
  0.0 96.2 jit_solution(12456714819031649325)
XLA Ops:
  0.0 1.4 %stage.1 = (bf16[2,8,2816]{2,1,0:T(8,128)(2,1)S(1)}, bf16[2,8,32768]{2,1,0:T(8,128)(2,1)S(1)}, f32[12,256]{1,0:T(8,128)S(1)}, s32[4,256]{1,0:T(4,128)S(1)}, s32[1024,128]{1,0:T(8,128)S(1)}) custom-call(bf16[2,8,32768]{2,1,0:T(8,128)(2,1)} %refs_0_.1, f32[12,256]{1,0:T(8,128)} %refs_1_.1, s32[4,128]{1,0:T(4,128)} %refs_2_.1, s32[4,256]{1,0:T(4,128)} %refs_3_.1), custom_call_target="tpu_custom_call" | custom-call | tf_op jit(solution)/shard_map/stage/pallas_call | solution.py:94
  1.4 3.4 %collective-permute-start = (bf16[2,8,2816]{2,1,0:T(8,128)(2,1)S(1)}, bf16[2,8,2816]{2,1,0:T(8,128)(2,1)S(1)}, u32[]{:S(2)}, u32[]{:S(2)}) collective-permute-start(bf16[2,8,2816]{2,1,0:T(8,128)(2,1)S(1)} %get-tuple-element.19), channel_id=1, source_target_pairs={{0,1},{1,2},{2,3},{4,5},{5,6},{6,7},{8,9},{9,10},{10,11},{12,13},{... | collective-permute-start | bytes 270344 | tf_op jit(solution)/shard_map/ppermute | solution.py:25
  4.8 1.6 %filter_body.1 = (f32[2,2,1024,128]{3,2,1,0:T(8,128)S(1)}, bf16[512,512]{1,0:T(8,128)(2,1)S(1)}) custom-call(bf16[2,8,32768]{2,1,0:T(8,128)(2,1)S(1)} %get-tuple-element.16.x_ref, f32[12,256]{1,0:T(8,128)S(1)} %get-tuple-element.17.taps_ref, bf16[512,512]{1,0:T(8,128)(2,1)} %constant.2.clone.table_ref), custom_call_target="tpu_custom_call" | custom-call | flops 12000000 | bytes 6000000 | tf_op jit(solution)/shard_map/filter_body/pallas_call | solution.py:162
  6.4 0.5 collective-permute-done.halo_ref
  6.9 1.0 %transform.1 = bf16[512,8,128]{2,1,0:T(8,128)(2,1)S(1)} custom-call(f32[2,2,1024,128]{3,2,1,0:T(8,128)S(1)} %get-tuple-element.18.body_ref, bf16[2,8,2816]{2,1,0:T(8,128)(2,1)S(1)} %collective-permute-done.halo_ref, bf16[2,8,32768]{2,1,0:T(8,128)(2,1)S(1)} %get-tuple-element.16.x_ref, f32[12,256]{1,0:T(8,128)S(1)} %get-tuple-element.17.taps_ref, ...), custom_call_target="tpu_custom_call" | custom-call | flops 540000000 | bytes 4000000 | tf_op jit(solution)/shard_map/transform/pallas_call | solution.py:212
  7.9 66.6 %all_to_all.5.refs_1_ = bf16[128,4,8,128]{3,2,1,0:T(8,128)(2,1)S(1)} all-to-all(bf16[128,4,8,128]{3,2,1,0:T(8,128)(2,1)S(1)} %bitcast.1), channel_id=1, replica_groups={{340,84,344,88,348,92,352,96,356,100,360,104,364,108,368,112,372,116,37..., dimensions={0} | all-to-all | bytes 2097152 | tf_op jit(solution)/shard_map/all_to_all | solution.py:47
  74.6 0.4 choose.3.refs_2_
  75.0 5.8 %collective-permute-start.1 = (bf16[4,256,128]{2,1,0:T(8,128)(2,1)S(1)}, bf16[4,256,128]{2,1,0:T(8,128)(2,1)S(1)}, u32[]{:S(2)}, u32[]{:S(2)}) collective-permute-start(bf16[4,256,128]{2,1,0:T(8,128)(2,1)S(1)} %choose.3.refs_2_), channel_id=1, source_target_pairs={{0,2},{1,3},{2,0},{3,1},{4,6},{5,7},{6,4},{7,5},{8,10},{9,11},{10,... | collective-permute-start | bytes 786440 | tf_op jit(solution)/shard_map/ppermute | solution.py:43
  80.9 0.7 choose.4
  81.6 3.0 %collective-permute-start.3 = (bf16[4,256,128]{2,1,0:T(8,128)(2,1)S(1)}, bf16[4,256,128]{2,1,0:T(8,128)(2,1)S(1)}, u32[]{:S(2)}, u32[]{:S(2)}) collective-permute-start(bf16[4,256,128]{2,1,0:T(8,128)(2,1)S(1)} %get-tuple-element.22), channel_id=1, source_target_pairs={{0,3},{1,2},{2,1},{3,0},{4,7},{5,6},{6,5},{7,4},{8,11},{9,10},{10,... | collective-permute-start | bytes 786440 | tf_op jit(solution)/shard_map/ppermute | solution.py:43
  84.6 1.9 %collective-permute-start.2 = (bf16[4,256,128]{2,1,0:T(8,128)(2,1)S(1)}, bf16[4,256,128]{2,1,0:T(8,128)(2,1)S(1)}, u32[]{:S(2)}, u32[]{:S(2)}) collective-permute-start(bf16[4,256,128]{2,1,0:T(8,128)(2,1)S(1)} %get-tuple-element.21.refs_2_), channel_id=1, source_target_pairs={{0,1},{1,0},{2,3},{3,2},{4,5},{5,4},{6,7},{7,6},{8,9},{9,8},{10,11... | collective-permute-start | bytes 786440 | tf_op jit(solution)/shard_map/ppermute | solution.py:43
  86.6 0.4 choose.5.refs_0_
  87.0 1.0 %collective-permute-done.1.refs_1_ = bf16[4,256,128]{2,1,0:T(8,128)(2,1)S(1)} collective-permute-done((bf16[4,256,128]{2,1,0:T(8,128)(2,1)S(1)}, bf16[4,256,128]{2,1,0:T(8,128)(2,1)S(1)}, u32[]{:S(2)}, u32[]{:S(2)}) %collective-permute-start.1) | collective-permute-done | bytes 262176 | tf_op jit(solution)/shard_map/ppermute | solution.py:43
  88.0 0.5 begin.1.begun_ref
  88.5 5.1 %collective-permute-done.3.refs_1_ = bf16[4,256,128]{2,1,0:T(8,128)(2,1)S(1)} collective-permute-done((bf16[4,256,128]{2,1,0:T(8,128)(2,1)S(1)}, bf16[4,256,128]{2,1,0:T(8,128)(2,1)S(1)}, u32[]{:S(2)}, u32[]{:S(2)}) %collective-permute-start.3) | collective-permute-done | bytes 262176 | tf_op jit(solution)/shard_map/ppermute | solution.py:43
  93.6 1.2 %collective-permute-done.2.refs_0_ = bf16[4,256,128]{2,1,0:T(8,128)(2,1)S(1)} collective-permute-done((bf16[4,256,128]{2,1,0:T(8,128)(2,1)S(1)}, bf16[4,256,128]{2,1,0:T(8,128)(2,1)S(1)}, u32[]{:S(2)}, u32[]{:S(2)}) %collective-permute-start.2) | collective-permute-done | bytes 262176 | tf_op jit(solution)/shard_map/ppermute | solution.py:43
  94.8 1.3 %correlate.1 = f32[1,2,2,256,256]{4,3,2,1,0:T(8,128)} custom-call(s32[4,256]{1,0:T(4,128)S(1)} %get-tuple-element.14.allocation_ref, f32[2,2,256,256]{3,2,1,0:T(8,128)S(1)} %begin.1.begun_ref, bf16[4,256,128]{2,1,0:T(8,128)(2,1)S(1)} %collective-permute-done.2.refs_0_, bf16[4,256,128]{2,1,0:T(8,128)(2,1)S(1)} %collective-permute-done.3.refs_1_), custom_call_target="tpu_custom_call" | custom-call | flops 270000000 | bytes 2000000 | tf_op jit(solution)/shard_map/correlate/pallas_call | solution.py:322
Async XLA Ops:
  1.4 5.5 %collective-permute-start = (bf16[2,8,2816]{2,1,0:T(8,128)(2,1)S(1)}, bf16[2,8,2816]{2,1,0:T(8,128)(2,1)S(1)}, u32[]{:S(2)}, u32[]{:S(2)}) collective-permute-start(bf16[2,8,2816]{2,1,0:T(8,128)(2,1)S(1)} %get-tuple-element.19), channel_id=1, source_target_pairs={{0,1},{1,2},{2,3},{4,5},{5,6},{6,7},{8,9},{9,10},{10,11},{12,13},{... | collective-permute-start | bytes 270344 | tf_op jit(solution)/shard_map/ppermute | solution.py:25
  75.0 13.0 %collective-permute-start.1 = (bf16[4,256,128]{2,1,0:T(8,128)(2,1)S(1)}, bf16[4,256,128]{2,1,0:T(8,128)(2,1)S(1)}, u32[]{:S(2)}, u32[]{:S(2)}) collective-permute-start(bf16[4,256,128]{2,1,0:T(8,128)(2,1)S(1)} %choose.3.refs_2_), channel_id=1, source_target_pairs={{0,2},{1,3},{2,0},{3,1},{4,6},{5,7},{6,4},{7,5},{8,10},{9,11},{10,... | collective-permute-start | bytes 786440 | tf_op jit(solution)/shard_map/ppermute | solution.py:43
  81.6 12.0 %collective-permute-start.3 = (bf16[4,256,128]{2,1,0:T(8,128)(2,1)S(1)}, bf16[4,256,128]{2,1,0:T(8,128)(2,1)S(1)}, u32[]{:S(2)}, u32[]{:S(2)}) collective-permute-start(bf16[4,256,128]{2,1,0:T(8,128)(2,1)S(1)} %get-tuple-element.22), channel_id=1, source_target_pairs={{0,3},{1,2},{2,1},{3,0},{4,7},{5,6},{6,5},{7,4},{8,11},{9,10},{10,... | collective-permute-start | bytes 786440 | tf_op jit(solution)/shard_map/ppermute | solution.py:43
  84.6 10.2 %collective-permute-start.2 = (bf16[4,256,128]{2,1,0:T(8,128)(2,1)S(1)}, bf16[4,256,128]{2,1,0:T(8,128)(2,1)S(1)}, u32[]{:S(2)}, u32[]{:S(2)}) collective-permute-start(bf16[4,256,128]{2,1,0:T(8,128)(2,1)S(1)} %get-tuple-element.21.refs_2_), channel_id=1, source_target_pairs={{0,1},{1,0},{2,3},{3,2},{4,5},{5,4},{6,7},{7,6},{8,9},{9,8},{10,11... | collective-permute-start | bytes 786440 | tf_op jit(solution)/shard_map/ppermute | solution.py:43

commit v7 on v6

--- a/solution.py
+++ b/solution.py
@@ -127,7 +127,7 @@
     return total
 
 
-def filter_kernel(x_ref, taps_ref, table_ref, out_ref, table_out, sem):
+def filter_kernel(x_ref, taps_ref, table_ref, out_ref, table_out, filtered, sem):
     copy = pltpu.make_async_copy(table_ref, table_out, sem)
     copy.start()
     taps, length = taps_ref.shape
@@ -145,13 +145,15 @@
                 ]
                 for frame in range(BLOCK):
                     total = filter_frame(weights, window[frame : frame + taps])
-                    out_ref[part, col, pl.ds(first + frame, signals, stride=frames), :] = total
+                    filtered[part, col, pl.ds(first + frame, signals, stride=frames), :] = total
                 return tuple(window[BLOCK:])
 
             opening = tuple(
                 load_frame(x_ref, part, BLOCK - (taps - 1) + frame, col, cols) for frame in range(taps - 1)
             )
             lax.fori_loop(1, frames // BLOCK, step, opening, unroll=frames // BLOCK - 1)
+            place = (part * cols + col) * LANES
+            out_ref[:, place : place + LANES] = filtered[part, col].astype(jnp.bfloat16)
     copy.wait()
 
 
@@ -163,8 +165,8 @@
         filter_kernel,
         in_specs=[IN_VMEM, IN_VMEM, IN_HBM],
         out_specs=[IN_VMEM] * 2,
-        out_shape=[pltpu.VMEM(shape, jnp.float32), pltpu.VMEM(table.shape, table.dtype)],
-        scratch_shapes=[pltpu.SemaphoreType.DMA(())],
+        out_shape=[pltpu.VMEM((shape[2], 2 * length), jnp.bfloat16), pltpu.VMEM(table.shape, table.dtype)],
+        scratch_shapes=[pltpu.VMEM(shape, jnp.float32), pltpu.SemaphoreType.DMA(())],
         compiler_params=PARAMS,
         cost_estimate=pl.CostEstimate(flops=12_000_000, bytes_accessed=6_000_000, transcendentals=0),
         name="filter_body",
@@ -187,15 +189,13 @@
 
     rows = table_ref.shape[0]
     for pair in range(0, signals, 2):
-        columns = []
-        for part in range(2):
-            for col in range(cols):
-                pieces = []
-                for signal in (pair, pair + 1):
-                    pieces.append(opening[part, col, signal * BLOCK : (signal + 1) * BLOCK, :])
-                    pieces.append(body_ref[part, col, signal * frames + BLOCK : (signal + 1) * frames, :])
-                columns.append(jnp.concatenate(pieces, axis=0))
-        samples = jnp.concatenate(columns, axis=1).astype(jnp.bfloat16)
+        pieces = []
+        for signal in (pair, pair + 1):
+            rows_of = slice(signal * BLOCK, (signal + 1) * BLOCK)
+            start = [opening[part, col, rows_of, :] for part in range(2) for col in range(cols)]
+            pieces.append(jnp.concatenate(start, axis=1).astype(jnp.bfloat16))
+            pieces.append(body_ref[signal * frames + BLOCK : (signal + 1) * frames, :])
+        samples = jnp.concatenate(pieces, axis=0)
         spectrum = lax.dot_general(table_ref[...], samples, CONTRACT_LAST, preferred_element_type=jnp.float32)
         for which in range(2):
             turned[pl.ds(pair + which, rows, stride=signals), :] = spectrum[

time: 96.4 us -> 96.4 us (level)
  transfers between devices with their start and end apart: 4 -> 4, of which waited for: 4 -> 4; matrix products, arithmetic and copies ran while one was open for 0% -> 0% of each run, Pallas kernels for 3% -> 4%
where the time goes in v7:
time: 96.4 us; the launch traced here: 96.1 us
  blocking collectives  66.7 us (69%)
  starting transfers between devices  14.2 us (15%)
  Pallas kernels  7.64 us (8%)
  waiting for transfers between devices  7.56 us (8%)
    all_to_all x1, blocking collectives, exchange(): lax.all_to_all(value, axis, split_axis=0, concat_axis=0, tiled=True, axis...  66.7 us
    ppermute x3, starting transfers between devices, paired(): lax.ppermute(value, axis, [(source, source ^ steps) for source in range(c...  10.8 us
    ppermute x3, waiting for transfers between devices, paired(): lax.ppermute(value, axis, [(source, source ^ steps) for source in range(c...  7.32 us
    ppermute x1, starting transfers between devices, shifted(): lax.ppermute(value, axis, [(source, source + steps) for source in range(i...  3.4 us
  transfers between devices with their start and end apart: 4, of which 4 were waited for; matrix products, arithmetic and copies ran while one was open for 0% of the time, Pallas kernels for 4%

profile of v7, /device:TPU:24, one launch (start us, length us, event | category | flops | bytes accessed | tf_op | source)
XLA Modules:
  0.0 96.1 jit_solution(17590248053960597817)
XLA Ops:
  0.0 1.4 %stage.1 = (bf16[2,8,2816]{2,1,0:T(8,128)(2,1)S(1)}, bf16[2,8,32768]{2,1,0:T(8,128)(2,1)S(1)}, f32[12,256]{1,0:T(8,128)S(1)}, s32[4,256]{1,0:T(4,128)S(1)}, s32[1024,128]{1,0:T(8,128)S(1)}) custom-call(bf16[2,8,32768]{2,1,0:T(8,128)(2,1)} %refs_0_.1, f32[12,256]{1,0:T(8,128)} %refs_1_.1, s32[4,128]{1,0:T(4,128)} %refs_2_.1, s32[4,256]{1,0:T(4,128)} %refs_3_.1), custom_call_target="tpu_custom_call" | custom-call | tf_op jit(solution)/shard_map/stage/pallas_call | solution.py:94
  1.4 3.4 %collective-permute-start = (bf16[2,8,2816]{2,1,0:T(8,128)(2,1)S(1)}, bf16[2,8,2816]{2,1,0:T(8,128)(2,1)S(1)}, u32[]{:S(2)}, u32[]{:S(2)}) collective-permute-start(bf16[2,8,2816]{2,1,0:T(8,128)(2,1)S(1)} %get-tuple-element.19), channel_id=1, source_target_pairs={{0,1},{1,2},{2,3},{4,5},{5,6},{6,7},{8,9},{9,10},{10,11},{12,13},{... | collective-permute-start | bytes 270344 | tf_op jit(solution)/shard_map/ppermute | solution.py:25
  4.8 1.9 %filter_body.1 = (bf16[1024,512]{1,0:T(8,128)(2,1)S(1)}, bf16[512,512]{1,0:T(8,128)(2,1)S(1)}) custom-call(bf16[2,8,32768]{2,1,0:T(8,128)(2,1)S(1)} %get-tuple-element.16.x_ref, f32[12,256]{1,0:T(8,128)S(1)} %get-tuple-element.17.taps_ref, bf16[512,512]{1,0:T(8,128)(2,1)} %constant.2.clone.table_ref), custom_call_target="tpu_custom_call" | custom-call | flops 12000000 | bytes 6000000 | tf_op jit(solution)/shard_map/filter_body/pallas_call | solution.py:164
  6.7 0.2 collective-permute-done.halo_ref
  6.9 1.0 %transform.1 = bf16[512,8,128]{2,1,0:T(8,128)(2,1)S(1)} custom-call(bf16[1024,512]{1,0:T(8,128)(2,1)S(1)} %get-tuple-element.18.body_ref, bf16[2,8,2816]{2,1,0:T(8,128)(2,1)S(1)} %collective-permute-done.halo_ref, bf16[2,8,32768]{2,1,0:T(8,128)(2,1)S(1)} %get-tuple-element.16.x_ref, f32[12,256]{1,0:T(8,128)S(1)} %get-tuple-element.17.taps_ref, ...), custom_call_target="tpu_custom_call" | custom-call | flops 540000000 | bytes 4000000 | tf_op jit(solution)/shard_map/transform/pallas_call | solution.py:212
  7.9 66.7 %all_to_all.5.refs_1_ = bf16[128,4,8,128]{3,2,1,0:T(8,128)(2,1)S(1)} all-to-all(bf16[128,4,8,128]{3,2,1,0:T(8,128)(2,1)S(1)} %bitcast.1), channel_id=1, replica_groups={{340,84,344,88,348,92,352,96,356,100,360,104,364,108,368,112,372,116,37..., dimensions={0} | all-to-all | bytes 2097152 | tf_op jit(solution)/shard_map/all_to_all | solution.py:47
  74.6 0.4 choose.3.refs_2_
  75.0 5.8 %collective-permute-start.1 = (bf16[4,256,128]{2,1,0:T(8,128)(2,1)S(1)}, bf16[4,256,128]{2,1,0:T(8,128)(2,1)S(1)}, u32[]{:S(2)}, u32[]{:S(2)}) collective-permute-start(bf16[4,256,128]{2,1,0:T(8,128)(2,1)S(1)} %choose.3.refs_2_), channel_id=1, source_target_pairs={{0,2},{1,3},{2,0},{3,1},{4,6},{5,7},{6,4},{7,5},{8,10},{9,11},{10,... | collective-permute-start | bytes 786440 | tf_op jit(solution)/shard_map/ppermute | solution.py:43
  80.9 0.7 choose.4
  81.6 3.0 %collective-permute-start.3 = (bf16[4,256,128]{2,1,0:T(8,128)(2,1)S(1)}, bf16[4,256,128]{2,1,0:T(8,128)(2,1)S(1)}, u32[]{:S(2)}, u32[]{:S(2)}) collective-permute-start(bf16[4,256,128]{2,1,0:T(8,128)(2,1)S(1)} %get-tuple-element.22), channel_id=1, source_target_pairs={{0,3},{1,2},{2,1},{3,0},{4,7},{5,6},{6,5},{7,4},{8,11},{9,10},{10,... | collective-permute-start | bytes 786440 | tf_op jit(solution)/shard_map/ppermute | solution.py:43
  84.6 1.9 %collective-permute-start.2 = (bf16[4,256,128]{2,1,0:T(8,128)(2,1)S(1)}, bf16[4,256,128]{2,1,0:T(8,128)(2,1)S(1)}, u32[]{:S(2)}, u32[]{:S(2)}) collective-permute-start(bf16[4,256,128]{2,1,0:T(8,128)(2,1)S(1)} %get-tuple-element.21.refs_2_), channel_id=1, source_target_pairs={{0,1},{1,0},{2,3},{3,2},{4,5},{5,4},{6,7},{7,6},{8,9},{9,8},{10,11... | collective-permute-start | bytes 786440 | tf_op jit(solution)/shard_map/ppermute | solution.py:43
  86.6 0.4 choose.5.refs_0_
  87.0 1.0 %collective-permute-done.1.refs_1_ = bf16[4,256,128]{2,1,0:T(8,128)(2,1)S(1)} collective-permute-done((bf16[4,256,128]{2,1,0:T(8,128)(2,1)S(1)}, bf16[4,256,128]{2,1,0:T(8,128)(2,1)S(1)}, u32[]{:S(2)}, u32[]{:S(2)}) %collective-permute-start.1) | collective-permute-done | bytes 262176 | tf_op jit(solution)/shard_map/ppermute | solution.py:43
  88.0 0.5 begin.1.begun_ref
  88.4 5.1 %collective-permute-done.3.refs_1_ = bf16[4,256,128]{2,1,0:T(8,128)(2,1)S(1)} collective-permute-done((bf16[4,256,128]{2,1,0:T(8,128)(2,1)S(1)}, bf16[4,256,128]{2,1,0:T(8,128)(2,1)S(1)}, u32[]{:S(2)}, u32[]{:S(2)}) %collective-permute-start.3) | collective-permute-done | bytes 262176 | tf_op jit(solution)/shard_map/ppermute | solution.py:43
  93.6 1.2 %collective-permute-done.2.refs_0_ = bf16[4,256,128]{2,1,0:T(8,128)(2,1)S(1)} collective-permute-done((bf16[4,256,128]{2,1,0:T(8,128)(2,1)S(1)}, bf16[4,256,128]{2,1,0:T(8,128)(2,1)S(1)}, u32[]{:S(2)}, u32[]{:S(2)}) %collective-permute-start.2) | collective-permute-done | bytes 262176 | tf_op jit(solution)/shard_map/ppermute | solution.py:43
  94.8 1.3 %correlate.1 = f32[1,2,2,256,256]{4,3,2,1,0:T(8,128)} custom-call(s32[4,256]{1,0:T(4,128)S(1)} %get-tuple-element.14.allocation_ref, f32[2,2,256,256]{3,2,1,0:T(8,128)S(1)} %begin.1.begun_ref, bf16[4,256,128]{2,1,0:T(8,128)(2,1)S(1)} %collective-permute-done.2.refs_0_, bf16[4,256,128]{2,1,0:T(8,128)(2,1)S(1)} %collective-permute-done.3.refs_1_), custom_call_target="tpu_custom_call" | custom-call | flops 270000000 | bytes 2000000 | tf_op jit(solution)/shard_map/correlate/pallas_call | solution.py:322
Async XLA Ops:
  1.4 5.5 %collective-permute-start = (bf16[2,8,2816]{2,1,0:T(8,128)(2,1)S(1)}, bf16[2,8,2816]{2,1,0:T(8,128)(2,1)S(1)}, u32[]{:S(2)}, u32[]{:S(2)}) collective-permute-start(bf16[2,8,2816]{2,1,0:T(8,128)(2,1)S(1)} %get-tuple-element.19), channel_id=1, source_target_pairs={{0,1},{1,2},{2,3},{4,5},{5,6},{6,7},{8,9},{9,10},{10,11},{12,13},{... | collective-permute-start | bytes 270344 | tf_op jit(solution)/shard_map/ppermute | solution.py:25
  75.0 12.9 %collective-permute-start.1 = (bf16[4,256,128]{2,1,0:T(8,128)(2,1)S(1)}, bf16[4,256,128]{2,1,0:T(8,128)(2,1)S(1)}, u32[]{:S(2)}, u32[]{:S(2)}) collective-permute-start(bf16[4,256,128]{2,1,0:T(8,128)(2,1)S(1)} %choose.3.refs_2_), channel_id=1, source_target_pairs={{0,2},{1,3},{2,0},{3,1},{4,6},{5,7},{6,4},{7,5},{8,10},{9,11},{10,... | collective-permute-start | bytes 786440 | tf_op jit(solution)/shard_map/ppermute | solution.py:43
  81.6 12.0 %collective-permute-start.3 = (bf16[4,256,128]{2,1,0:T(8,128)(2,1)S(1)}, bf16[4,256,128]{2,1,0:T(8,128)(2,1)S(1)}, u32[]{:S(2)}, u32[]{:S(2)}) collective-permute-start(bf16[4,256,128]{2,1,0:T(8,128)(2,1)S(1)} %get-tuple-element.22), channel_id=1, source_target_pairs={{0,3},{1,2},{2,1},{3,0},{4,7},{5,6},{6,5},{7,4},{8,11},{9,10},{10,... | collective-permute-start | bytes 786440 | tf_op jit(solution)/shard_map/ppermute | solution.py:43
  84.6 10.2 %collective-permute-start.2 = (bf16[4,256,128]{2,1,0:T(8,128)(2,1)S(1)}, bf16[4,256,128]{2,1,0:T(8,128)(2,1)S(1)}, u32[]{:S(2)}, u32[]{:S(2)}) collective-permute-start(bf16[4,256,128]{2,1,0:T(8,128)(2,1)S(1)} %get-tuple-element.21.refs_2_), channel_id=1, source_target_pairs={{0,1},{1,0},{2,3},{3,2},{4,5},{5,4},{6,7},{7,6},{8,9},{9,8},{10,11... | collective-permute-start | bytes 786440 | tf_op jit(solution)/shard_map/ppermute | solution.py:43

commit v8 on v6

--- a/solution.py
+++ b/solution.py
@@ -356,7 +356,7 @@
     for blocks in ORDER:
         after = choose(places, turned, members, blocks, after[:1])
         met += [paired(value, "tm", block) if block else value for block, value in zip(blocks, after)]
-    return correlate(allocation, begin([met[-1], met[0]]), met[1:-1])
+    return correlate(allocation, begin([met[-1], met[0], met[2]]), met[1:2])
 
 
 def solution(mesh):

time: 96.4 us -> 96.7 us (level)
  transfers between devices with their start and end apart: 4 -> 4, of which waited for: 4 -> 4; matrix products, arithmetic and copies ran while one was open for 0% -> 0% of each run, Pallas kernels for 3% -> 4%
where the time goes in v8:
time: 96.7 us; the launch traced here: 96.1 us
  blocking collectives  66.6 us (69%)
  starting transfers between devices  14.2 us (15%)
  waiting for transfers between devices  7.67 us (8%)
  Pallas kernels  7.47 us (8%)
    all_to_all x1, blocking collectives, exchange(): lax.all_to_all(value, axis, split_axis=0, concat_axis=0, tiled=True, axis...  66.6 us
    ppermute x3, starting transfers between devices, paired(): lax.ppermute(value, axis, [(source, source ^ steps) for source in range(c...  10.8 us
    ppermute x3, waiting for transfers between devices, paired(): lax.ppermute(value, axis, [(source, source ^ steps) for source in range(c...  7.19 us
    ppermute x1, starting transfers between devices, shifted(): lax.ppermute(value, axis, [(source, source + steps) for source in range(i...  3.4 us
  transfers between devices with their start and end apart: 4, of which 4 were waited for; matrix products, arithmetic and copies ran while one was open for 0% of the time, Pallas kernels for 4%

profile of v8, /device:TPU:24, one launch (start us, length us, event | category | flops | bytes accessed | tf_op | source)
XLA Modules:
  0.0 96.1 jit_solution(14290586713100122298)
XLA Ops:
  0.0 1.4 %stage.1 = (bf16[2,8,2816]{2,1,0:T(8,128)(2,1)S(1)}, bf16[2,8,32768]{2,1,0:T(8,128)(2,1)S(1)}, f32[12,256]{1,0:T(8,128)S(1)}, s32[4,256]{1,0:T(4,128)S(1)}, s32[1024,128]{1,0:T(8,128)S(1)}) custom-call(bf16[2,8,32768]{2,1,0:T(8,128)(2,1)} %refs_0_.1, f32[12,256]{1,0:T(8,128)} %refs_1_.1, s32[4,128]{1,0:T(4,128)} %refs_2_.1, s32[4,256]{1,0:T(4,128)} %refs_3_.1), custom_call_target="tpu_custom_call" | custom-call | tf_op jit(solution)/shard_map/stage/pallas_call | solution.py:94
  1.4 3.4 %collective-permute-start = (bf16[2,8,2816]{2,1,0:T(8,128)(2,1)S(1)}, bf16[2,8,2816]{2,1,0:T(8,128)(2,1)S(1)}, u32[]{:S(2)}, u32[]{:S(2)}) collective-permute-start(bf16[2,8,2816]{2,1,0:T(8,128)(2,1)S(1)} %get-tuple-element.19), channel_id=1, source_target_pairs={{0,1},{1,2},{2,3},{4,5},{5,6},{6,7},{8,9},{9,10},{10,11},{12,13},{... | collective-permute-start | bytes 270344 | tf_op jit(solution)/shard_map/ppermute | solution.py:25
  4.8 1.6 %filter_body.1 = (f32[2,2,1024,128]{3,2,1,0:T(8,128)S(1)}, bf16[512,512]{1,0:T(8,128)(2,1)S(1)}) custom-call(bf16[2,8,32768]{2,1,0:T(8,128)(2,1)S(1)} %get-tuple-element.16.x_ref, f32[12,256]{1,0:T(8,128)S(1)} %get-tuple-element.17.taps_ref, bf16[512,512]{1,0:T(8,128)(2,1)} %constant.2.clone.table_ref), custom_call_target="tpu_custom_call" | custom-call | flops 12000000 | bytes 6000000 | tf_op jit(solution)/shard_map/filter_body/pallas_call | solution.py:162
  6.4 0.5 collective-permute-done.halo_ref
  6.9 1.0 %transform.1 = bf16[512,8,128]{2,1,0:T(8,128)(2,1)S(1)} custom-call(f32[2,2,1024,128]{3,2,1,0:T(8,128)S(1)} %get-tuple-element.18.body_ref, bf16[2,8,2816]{2,1,0:T(8,128)(2,1)S(1)} %collective-permute-done.halo_ref, bf16[2,8,32768]{2,1,0:T(8,128)(2,1)S(1)} %get-tuple-element.16.x_ref, f32[12,256]{1,0:T(8,128)S(1)} %get-tuple-element.17.taps_ref, ...), custom_call_target="tpu_custom_call" | custom-call | flops 540000000 | bytes 4000000 | tf_op jit(solution)/shard_map/transform/pallas_call | solution.py:212
  7.9 66.6 %all_to_all.5.refs_1_ = bf16[128,4,8,128]{3,2,1,0:T(8,128)(2,1)S(1)} all-to-all(bf16[128,4,8,128]{3,2,1,0:T(8,128)(2,1)S(1)} %bitcast.1), channel_id=1, replica_groups={{340,84,344,88,348,92,352,96,356,100,360,104,364,108,368,112,372,116,37..., dimensions={0} | all-to-all | bytes 2097152 | tf_op jit(solution)/shard_map/all_to_all | solution.py:47
  74.6 0.4 choose.3.refs_2_
  75.0 5.8 %collective-permute-start.1 = (bf16[4,256,128]{2,1,0:T(8,128)(2,1)S(1)}, bf16[4,256,128]{2,1,0:T(8,128)(2,1)S(1)}, u32[]{:S(2)}, u32[]{:S(2)}) collective-permute-start(bf16[4,256,128]{2,1,0:T(8,128)(2,1)S(1)} %choose.3.refs_2_), channel_id=1, source_target_pairs={{0,2},{1,3},{2,0},{3,1},{4,6},{5,7},{6,4},{7,5},{8,10},{9,11},{10,... | collective-permute-start | bytes 786440 | tf_op jit(solution)/shard_map/ppermute | solution.py:43
  80.9 0.7 choose.4
  81.6 3.0 %collective-permute-start.2 = (bf16[4,256,128]{2,1,0:T(8,128)(2,1)S(1)}, bf16[4,256,128]{2,1,0:T(8,128)(2,1)S(1)}, u32[]{:S(2)}, u32[]{:S(2)}) collective-permute-start(bf16[4,256,128]{2,1,0:T(8,128)(2,1)S(1)} %get-tuple-element.22), channel_id=1, source_target_pairs={{0,3},{1,2},{2,1},{3,0},{4,7},{5,6},{6,5},{7,4},{8,11},{9,10},{10,... | collective-permute-start | bytes 786440 | tf_op jit(solution)/shard_map/ppermute | solution.py:43
  84.6 1.9 %collective-permute-start.3 = (bf16[4,256,128]{2,1,0:T(8,128)(2,1)S(1)}, bf16[4,256,128]{2,1,0:T(8,128)(2,1)S(1)}, u32[]{:S(2)}, u32[]{:S(2)}) collective-permute-start(bf16[4,256,128]{2,1,0:T(8,128)(2,1)S(1)} %get-tuple-element.21.refs_2_), channel_id=1, source_target_pairs={{0,1},{1,0},{2,3},{3,2},{4,5},{5,4},{6,7},{7,6},{8,9},{9,8},{10,11... | collective-permute-start | bytes 786440 | tf_op jit(solution)/shard_map/ppermute | solution.py:43
  86.6 0.4 choose.5.refs_0_
  87.0 1.0 %collective-permute-done.1.refs_1_ = bf16[4,256,128]{2,1,0:T(8,128)(2,1)S(1)} collective-permute-done((bf16[4,256,128]{2,1,0:T(8,128)(2,1)S(1)}, bf16[4,256,128]{2,1,0:T(8,128)(2,1)S(1)}, u32[]{:S(2)}, u32[]{:S(2)}) %collective-permute-start.1) | collective-permute-done | bytes 262176 | tf_op jit(solution)/shard_map/ppermute | solution.py:43
  88.0 5.6 %collective-permute-done.2.refs_2_ = bf16[4,256,128]{2,1,0:T(8,128)(2,1)S(1)} collective-permute-done((bf16[4,256,128]{2,1,0:T(8,128)(2,1)S(1)}, bf16[4,256,128]{2,1,0:T(8,128)(2,1)S(1)}, u32[]{:S(2)}, u32[]{:S(2)}) %collective-permute-start.2) | collective-permute-done | bytes 262176 | tf_op jit(solution)/shard_map/ppermute | solution.py:43
  93.6 0.6 begin.1.begun_ref
  94.2 0.6 collective-permute-done.3.refs_0_
  94.8 1.3 %correlate.1 = f32[1,2,2,256,256]{4,3,2,1,0:T(8,128)} custom-call(s32[4,256]{1,0:T(4,128)S(1)} %get-tuple-element.14.allocation_ref, f32[2,2,256,256]{3,2,1,0:T(8,128)S(1)} %begin.1.begun_ref, bf16[4,256,128]{2,1,0:T(8,128)(2,1)S(1)} %collective-permute-done.3.refs_0_), custom_call_target="tpu_custom_call" | custom-call | flops 270000000 | bytes 2000000 | tf_op jit(solution)/shard_map/correlate/pallas_call | solution.py:322
Async XLA Ops:
  1.4 5.5 %collective-permute-start = (bf16[2,8,2816]{2,1,0:T(8,128)(2,1)S(1)}, bf16[2,8,2816]{2,1,0:T(8,128)(2,1)S(1)}, u32[]{:S(2)}, u32[]{:S(2)}) collective-permute-start(bf16[2,8,2816]{2,1,0:T(8,128)(2,1)S(1)} %get-tuple-element.19), channel_id=1, source_target_pairs={{0,1},{1,2},{2,3},{4,5},{5,6},{6,7},{8,9},{9,10},{10,11},{12,13},{... | collective-permute-start | bytes 270344 | tf_op jit(solution)/shard_map/ppermute | solution.py:25
  75.0 13.0 %collective-permute-start.1 = (bf16[4,256,128]{2,1,0:T(8,128)(2,1)S(1)}, bf16[4,256,128]{2,1,0:T(8,128)(2,1)S(1)}, u32[]{:S(2)}, u32[]{:S(2)}) collective-permute-start(bf16[4,256,128]{2,1,0:T(8,128)(2,1)S(1)} %choose.3.refs_2_), channel_id=1, source_target_pairs={{0,2},{1,3},{2,0},{3,1},{4,6},{5,7},{6,4},{7,5},{8,10},{9,11},{10,... | collective-permute-start | bytes 786440 | tf_op jit(solution)/shard_map/ppermute | solution.py:43
  81.6 12.0 %collective-permute-start.2 = (bf16[4,256,128]{2,1,0:T(8,128)(2,1)S(1)}, bf16[4,256,128]{2,1,0:T(8,128)(2,1)S(1)}, u32[]{:S(2)}, u32[]{:S(2)}) collective-permute-start(bf16[4,256,128]{2,1,0:T(8,128)(2,1)S(1)} %get-tuple-element.22), channel_id=1, source_target_pairs={{0,3},{1,2},{2,1},{3,0},{4,7},{5,6},{6,5},{7,4},{8,11},{9,10},{10,... | collective-permute-start | bytes 786440 | tf_op jit(solution)/shard_map/ppermute | solution.py:43
  84.6 10.2 %collective-permute-start.3 = (bf16[4,256,128]{2,1,0:T(8,128)(2,1)S(1)}, bf16[4,256,128]{2,1,0:T(8,128)(2,1)S(1)}, u32[]{:S(2)}, u32[]{:S(2)}) collective-permute-start(bf16[4,256,128]{2,1,0:T(8,128)(2,1)S(1)} %get-tuple-element.21.refs_2_), channel_id=1, source_target_pairs={{0,1},{1,0},{2,3},{3,2},{4,5},{5,4},{6,7},{7,6},{8,9},{9,8},{10,11... | collective-permute-start | bytes 786440 | tf_op jit(solution)/shard_map/ppermute | solution.py:43
